TPU v7x, 512 devices: a whole 4x8x8 slice. The times are simulated.
512 devices in a mesh: role: 4 (over y_lo), dp: 32 (over z, y_hi, core), mp: 4 (over x).
Axes of the slice: x: 4, y: 8 (y_hi: 2, y_lo: 4; y = y_hi * 4 + y_lo), z: 8, core: 2. Of those that a mesh axis runs over, the one named last changes fastest.
Arguments:
- residual_in: bfloat16 [4096, 8, 2048], P(('role', 'dp'), None, 'mp'), may hold values from -6 to 6
- context: bfloat16 [4096, 8, 2048], P(('role', 'dp'), None, 'mp'), may hold values from -6 to 6
- w_out: bfloat16 [2048, 2048], P('dp', 'mp'), may hold values from -0.125 to 0.125
- norm_gain: float32 [2048], P('mp'), may hold values from 0.1 to 1.9
- policy_head: bfloat16 [2048, 43], P('mp'), may hold values from -0.125 to 0.125
- value_head: bfloat16 [2048], P('mp'), may hold values from -0.125 to 0.125
- rewards: bfloat16 [4096, 8], P(('role', 'dp')), may hold values from -12 to 12
- resets: int32 [4096, 8], P(('role', 'dp')), may hold values 0 or 1
- actions: int32 [4096, 8], P(('role', 'dp')), may hold values from 0 to 42
- lengths: int32 [4096], P(('role', 'dp')), may hold values from 1 to 7
- assignment: int32 [4096], P(('role', 'dp')), may hold values from 0 to 31, as said below
Outputs:
- advantages: float32 [4096, 8], P(('role', 'dp'))
- adv_means: float32 [32], P('dp')
- grad_w: float32 [2048, 2048], P('dp', 'mp')
- grad_gain: float32 [2048], P('mp')
- grad_policy: float32 [2048, 43], P('mp')
- grad_value: float32 [2048], P('mp')
Inputs may be any that keep to these rules, and one draw needn't show every extreme that they name: `assignment`: each device sends either none or exactly 2 of its environments to each learner index, and each learner index receives exactly 32 environments from the devices of each group. `lengths`: rows 0 to length - 1 of an environment are its trajectory; row length is the observation that bootstraps it.
All inputs are finite; a program needn't handle non-finite values. No bound on the sum of `resets` on one device may be relied on, other than what follows from the above.
Results may differ from a plain program's by a relative error of at most 0.0027.
Values may be sent and summed in bfloat16 or wider, within the bound.
A program may use at most 64 MiB of HBM per device.

v0:
```python
import jax
import jax.numpy as jnp
from jax import lax
from jax.sharding import PartitionSpec as P

D = 2048


discount = 0.99
trace_decay = 0.95
value_weight = 0.5
epsilon = 1e-05
highest = lax.Precision.HIGHEST


def advantage_estimate(rewards, resets, values, lengths):
    num_env, num_steps = values.shape
    valid = (jnp.arange(num_steps)[None, :] < lengths[:, None]).astype(jnp.float32)
    next_values = jnp.concatenate([values[:, 1:], jnp.zeros((num_env, 1), jnp.float32)], axis=1)
    carry_on = 1.0 - resets.astype(jnp.float32)
    deltas = rewards.astype(jnp.float32) + discount * carry_on * next_values - values

    def step_back(later, inputs):
        delta_now, keep_now, valid_now = inputs
        current = valid_now * (delta_now + discount * trace_decay * keep_now * later)
        return (current, current)

    final_carry, stacked = lax.scan(
        step_back, jnp.zeros((num_env,), jnp.float32), (deltas.T, carry_on.T, valid.T), reverse=True
    )
    return (stacked.T, valid)


def forward(resid_cols, context_cols, weights, gain, policy, value_vec):
    num_env, num_steps, width_cols = context_cols.shape
    context_full = lax.all_gather(context_cols, "mp", axis=2, tiled=True)
    context_full = context_full.reshape(num_env * num_steps, -1)
    stream = resid_cols.reshape(num_env * num_steps, width_cols).astype(jnp.float32) + jnp.dot(
        context_full, weights, preferred_element_type=jnp.float32
    )
    squares = lax.psum(jnp.sum(stream * stream, axis=1), "mp")
    inverse = lax.rsqrt(squares / D + epsilon)
    normed = stream * inverse[:, None] * gain
    logits, values = lax.psum(
        (jnp.dot(normed, policy, precision=highest), jnp.dot(normed, value_vec, precision=highest)),
        "mp",
    )
    return (stream, inverse, context_full, logits, values)


def backward(
    stream, inverse, logits, values, actions, centered, returns, weight, gain, policy, value_vec
):
    log_probs = logits - jnp.log(jnp.sum(jnp.exp(logits), axis=1, keepdims=True))
    chosen = (actions[:, None] == jnp.arange(logits.shape[1])[None, :]).astype(jnp.float32)
    grad_logits = (weight * centered)[:, None] * (jnp.exp(log_probs) - chosen)
    grad_values = value_weight * weight * (values - returns)
    normed = stream * inverse[:, None] * gain
    grad_normed = (
        jnp.dot(grad_logits, policy.T, precision=highest) + grad_values[:, None] * value_vec
    )
    policy_grad = jnp.dot(normed.T, grad_logits, precision=highest)
    value_grad = jnp.dot(grad_values, normed, precision=highest)
    gain_grad = jnp.sum(grad_normed * stream * inverse[:, None], axis=0)
    inner = lax.psum(jnp.sum(grad_normed * gain * stream, axis=1), "mp")
    grad_stream = (
        inverse[:, None] * gain * grad_normed
        - stream * (inverse * inverse * inverse * inner / D)[:, None]
    )
    return (grad_stream.astype(jnp.bfloat16), policy_grad, value_grad, gain_grad)


def select_rows(selector, bulk, extras, integers):
    bulk_rows = jnp.dot(
        selector.astype(jnp.bfloat16), bulk, preferred_element_type=jnp.float32
    ).astype(jnp.bfloat16)
    extra_rows = jnp.dot(
        selector.astype(jnp.bfloat16), extras, preferred_element_type=jnp.float32
    ).astype(jnp.bfloat16)
    integer_rows = jnp.dot(selector.astype(jnp.int32), integers, preferred_element_type=jnp.int32)
    return (bulk_rows, extra_rows, integer_rows)


def compact_slots(bulk, extras, integers, keep_count):
    occupied = integers[:, -1] > 0
    ranking = jnp.cumsum(occupied.astype(jnp.int32)) - 1
    target = jnp.where(occupied, ranking, -1)
    selector = jnp.arange(keep_count)[:, None] == target[None, :]
    return select_rows(selector, bulk, extras, integers)


def per_device(
    residual_in,
    context,
    w_out,
    norm_gain,
    policy_head,
    value_head,
    rewards,
    resets,
    actions,
    lengths,
    assignment,
):
    num_env, num_steps, width_cols = context.shape
    learners = lax.axis_size("dp")
    most_slots = max(2, num_env // learners)
    weights = lax.all_gather(w_out, "dp", axis=0, tiled=True)
    policy = policy_head.astype(jnp.float32)
    value_vec = value_head.astype(jnp.float32)
    stream, inverse, context_full, logits, values = forward(
        residual_in, context, weights, norm_gain, policy, value_vec
    )
    value_grid = values.reshape(num_env, num_steps)
    advantages, valid = advantage_estimate(rewards, resets, value_grid, lengths)
    bulk = jnp.concatenate([context, residual_in], axis=2).reshape(num_env, -1)
    integers = jnp.concatenate([resets, actions, lengths[:, None]], axis=1)
    target_hit = (assignment[:, None] == jnp.arange(learners)[None, :]).astype(jnp.int32)
    position = jnp.sum(target_hit * (jnp.cumsum(target_hit, axis=0) - 1), axis=1)
    slot_index = assignment * most_slots + position
    selector = jnp.arange(learners * most_slots)[:, None] == slot_index[None, :]
    send_bulk, send_extras, send_ints = select_rows(selector, bulk, rewards, integers)
    send_bulk = send_bulk.reshape(learners, most_slots, -1)
    send_extras = send_extras.reshape(learners, most_slots, -1)
    send_ints = send_ints.reshape(learners, most_slots, -1)
    got_bulk, got_extras, got_ints = (
        lax.all_to_all(send_bulk, "dp", split_axis=0, concat_axis=0, tiled=True),
        lax.all_to_all(send_extras, "dp", split_axis=0, concat_axis=0, tiled=True),
        lax.all_to_all(send_ints, "dp", split_axis=0, concat_axis=0, tiled=True),
    )
    got_bulk = got_bulk.reshape(learners * most_slots, -1)
    got_extras = got_extras.reshape(learners * most_slots, -1)
    got_ints = got_ints.reshape(learners * most_slots, -1)
    every_bulk, every_extras, every_ints = (
        lax.all_gather(got_bulk, "role", axis=0, tiled=True),
        lax.all_gather(got_extras, "role", axis=0, tiled=True),
        lax.all_gather(got_ints, "role", axis=0, tiled=True),
    )
    rows_bulk, rows_extras, rows_ints = compact_slots(
        every_bulk, every_extras, every_ints, lax.axis_size("role") * num_env
    )
    held = rows_bulk.shape[0]
    rows_bulk = rows_bulk.reshape(held, num_steps, 2 * width_cols)
    learn_stream, learn_inverse, learn_context, learn_logits, learn_values = forward(
        rows_bulk[:, :, width_cols:],
        rows_bulk[:, :, :width_cols],
        weights,
        norm_gain,
        policy,
        value_vec,
    )
    held_resets = rows_ints[:, :num_steps]
    held_actions = rows_ints[:, num_steps : 2 * num_steps]
    held_lengths = rows_ints[:, 2 * num_steps]
    held_values = learn_values.reshape(held, num_steps)
    held_adv, held_valid = advantage_estimate(rows_extras, held_resets, held_values, held_lengths)
    held_returns = held_adv + held_values
    total = jnp.sum(held_valid)
    mean_adv = jnp.sum(held_adv) / total
    centered = (held_adv - mean_adv).reshape(-1)
    weight = (held_valid / total).reshape(-1)
    grad_stream, policy_grad, value_grad, gain_grad = backward(
        learn_stream,
        learn_inverse,
        learn_logits,
        learn_values,
        held_actions.reshape(-1),
        centered,
        held_returns.reshape(-1),
        weight,
        norm_gain,
        policy,
        value_vec,
    )
    adv_means = mean_adv.reshape(1)
    grad_w = lax.psum_scatter(
        lax.dot_general(
            learn_context, grad_stream, (((0,), (0,)), ((), ())), preferred_element_type=jnp.float32
        ),
        "dp",
        scatter_dimension=0,
        tiled=True,
    )
    policy_grad, value_grad, gain_grad = lax.psum((policy_grad, value_grad, gain_grad), "dp")
    return (advantages, adv_means, grad_w, gain_grad, policy_grad, value_grad)


def solution(mesh):
    placed = (
        P(("role", "dp"), None, "mp"),
        P(("role", "dp"), None, "mp"),
        P("dp", "mp"),
        P("mp"),
        P("mp", None),
        P("mp"),
        P(("role", "dp"), None),
        P(("role", "dp"), None),
        P(("role", "dp"), None),
        P(("role", "dp")),
        P(("role", "dp")),
    )
    return jax.shard_map(
        per_device,
        mesh=mesh,
        in_specs=placed,
        out_specs=(
            P(("role", "dp"), None),
            P("dp"),
            P("dp", "mp"),
            P("mp"),
            P("mp", None),
            P("mp"),
        ),
        check_vma=False,
    )
```

profile of v0, /device:TPU:1, one launch (start us, length us, event | category | flops | bytes accessed | tf_op | source)
XLA Modules:
  0.0 882.5 jit_solution(9423955281115027107)
XLA Ops:
  12.0 47.5 %all_to_all.15 = bf16[32,2,8192]{2,1,0:T(2,128)(2,1)S(1)} all-to-all(bf16[32,2,8192]{2,1,0:T(2,128)(2,1)S(1)} %reshape.152), channel_id=1, replica_groups=mesh['role'=4,'dp'=32,'mp'=4] {'dp'}, dimensions={0} | all-to-all | bytes 2097152 | tf_op jit(solution)/shard_map/all_to_all | solution.py:127
  62.5 18.3 %all_to_all.16 = s32[32,2,17]{2,1,0:T(2,128)S(1)} all-to-all(s32[32,2,17]{2,1,0:T(2,128)S(1)} %bitcast.126), channel_id=1, replica_groups=mesh['role'=4,'dp'=32,'mp'=4] {'dp'}, dimensions={0} | all-to-all | bytes 8704 | tf_op jit(solution)/shard_map/all_to_all | solution.py:129
  80.9 12.9 %all-gather = s32[4,64,17]{1,2,0:T(8,128)S(1)} all-gather(s32[1,64,17]{1,2,0:T(8,128)S(1)} %copy.80), channel_id=1, replica_groups=mesh['role'=4,'dp'=32,'mp'=4] {'role'}, dimensions={0}, use_global_device_ids=true | all-gather | bytes 21760 | tf_op jit(solution)/shard_map/all_gather | solution.py:137
  94.6 50.9 %all-gather.11.cloned.1.call-done = bf16[256,8192]{1,0:T(8,128)(2,1)} async-done(((bf16[64,8192]{1,0:T(8,128)(2,1)}), bf16[256,8192]{1,0:T(8,128)(2,1)}) %all-gather.11.cloned.1.call-update) | async-done | bytes 4194320 | tf_op jit(solution)/shard_map/all_gather | solution.py:135
  145.5 2.9 convolution_convert_fusion
  152.1 11.7 %all-to-all-start.1 = ((bf16[32,2,8]{2,1,0:T(2,128)(2,1)}), bf16[32,2,8]{2,1,0:T(2,128)(2,1)S(1)}, u32[]{:S(2)}, u32[]{:S(2)}) async-start(bf16[32,2,8]{2,1,0:T(2,128)(2,1)} %bitcast.12), calls=%async_computation.1 | async-start | bytes 32768 | tf_op jit(solution)/shard_map/all_to_all | solution.py:128
  163.9 11.6 %all-to-all-done.1 = bf16[32,2,8]{2,1,0:T(2,128)(2,1)S(1)} async-done(((bf16[32,2,8]{2,1,0:T(2,128)(2,1)}), bf16[32,2,8]{2,1,0:T(2,128)(2,1)S(1)}, u32[]{:S(2)}, u32[]{:S(2)}) %all-to-all-start.1) | async-done | bytes 1056 | tf_op jit(solution)/shard_map/all_to_all | solution.py:128
  175.5 9.3 %all-gather.1 = bf16[4,64,8]{1,2,0:T(8,128)(2,1)S(1)} all-gather(bf16[1,64,8]{1,2,0:T(8,128)(2,1)S(1)} %copy.83), channel_id=1, replica_groups=mesh['role'=4,'dp'=32,'mp'=4] {'role'}, dimensions={0}, use_global_device_ids=true | all-gather | bytes 5120 | tf_op jit(solution)/shard_map/all_gather | solution.py:136
  186.8 85.0 %all-gather.9.cloned.1.call-done = bf16[2048,512]{1,0:T(8,128)(2,1)} async-done(((bf16[64,512]{1,0:T(8,128)(2,1)}), bf16[2048,512]{1,0:T(8,128)(2,1)}) %all-gather.9.cloned.1.call-update) | async-done | bytes 2097168 | tf_op jit(solution)/shard_map/all_gather | solution.py:108
  271.8 2.7 multiply_reduce_fusion.3
  274.5 1.8 copy.85
  276.3 47.4 %all-gather.13.cloned.1.call-done = bf16[128,8,2048]{2,1,0:T(8,128)(2,1)} async-done(((bf16[128,8,512]{2,1,0:T(8,128)(2,1)}), bf16[128,8,2048]{2,1,0:T(8,128)(2,1)}) %all-gather.13.cloned.1.call-update) | async-done | bytes 4194320 | tf_op jit(solution)/shard_map/all_gather | solution.py:36
  323.7 5.8 multiply_reduce_fusion.2
  329.5 6.6 psum.65
  337.1 7.1 all-reduce.4
  350.0 52.9 %all-reduce.8.cloned.1.call-done = f32[1024,43]{0,1:T(8,128)} async-done(((f32[1024,43]{0,1:T(8,128)}), f32[1024,43]{0,1:T(8,128)}) %all-reduce.8.cloned.1.call-update) | async-done | bytes 176144 | tf_op jit(solution)/shard_map/psum | solution.py:44
  404.0 3.9 fusion.22
  407.9 3.0 multiply_reduce_fusion
  410.9 7.6 all-reduce.3
  418.6 7.4 fusion.14
  426.0 1.8 fusion.21
  427.9 90.0 %all-reduce.2 = (f32[512]{0:T(512)}, f32[512]{0:T(512)}) all-reduce(f32[512]{0:T(512)S(1)} %get-tuple-element.318, f32[512]{0:T(512)S(1)} %bitcast.132), channel_id=1, replica_groups=mesh['role'=4,'dp'=32,'mp'=4] {'dp'}, use_global_device_ids=true, to_apply=%region_22.23 | all-reduce | flops 1024 | bytes 8192 | tf_op jit(solution)/shard_map/psum | solution.py:184
  518.5 205.4 %all-reduce.10.cloned.1.call-done = f32[512,43]{0,1:T(8,128)} async-done(((f32[512,43]{0,1:T(8,128)}), f32[512,43]{0,1:T(8,128)}) %all-reduce.10.cloned.1.call-update) | async-done | bytes 88080 | tf_op jit(solution)/shard_map/psum | solution.py:184
  723.9 149.1 %reduce-scatter.2.cloned.1.call-done = f32[64,512]{1,0:T(8,128)} async-done(((f32[2048,512]{1,0:T(8,128)}), f32[64,512]{1,0:T(8,128)}) %reduce-scatter.2.cloned.1.call-update) | async-done | bytes 131088 | tf_op jit(solution)/shard_map/reduce_scatter | solution.py:176
  (134 shorter events, 23.1 us)
Async XLA Ops:
  7.2 340.2 %copy-start = (bf16[512,43]{0,1:T(8,128)(2,1)S(1)}, bf16[512,43]{0,1:T(8,128)(2,1)}, u32[]{:S(2)}) copy-start(bf16[512,43]{0,1:T(8,128)(2,1)} %param.19) | copy-start | bytes 132100
  7.2 138.3 %all-gather.11.cloned.1.call-start = ((), (), s32[]{:S(2)}) async-start(), calls=%async_computation.6 | async-start | bytes 5242880 | tf_op jit(solution)/shard_map/all_gather | solution.py:135
  59.5 2.8 copy-start.4
  59.6 2.8 copy-start.7
  59.6 2.8 copy-start.8
  60.8 126.0 %all-gather.7.cloned.1.call-start = ((), (), s32[]{:S(2)}) async-start(), calls=%async_computation.4 | async-start | bytes 1310720 | tf_op jit(solution)/shard_map/all_gather | solution.py:36
  61.6 210.2 %all-gather.9.cloned.1.call-start = ((), (), s32[]{:S(2)}) async-start(), calls=%async_computation.5 | async-start | bytes 2162688 | tf_op jit(solution)/shard_map/all_gather | solution.py:108
  62.3 261.4 %all-gather.13.cloned.1.call-start = ((), (), s32[]{:S(2)}) async-start(), calls=%async_computation.7 | async-start | bytes 5242880 | tf_op jit(solution)/shard_map/all_gather | solution.py:36
  149.8 1.4 copy-start.9
  149.9 14.0 %copy-start.5 = (bf16[512]{0:T(512)(128)(2,1)S(1)}, bf16[512]{0:T(512)(128)(2,1)}, u32[]{:S(2)}) copy-start(bf16[512]{0:T(512)(128)(2,1)} %param.20) | copy-start | bytes 3076
  149.9 121.9 %copy-start.2 = (bf16[32,8,512]{2,1,0:T(8,128)(2,1)S(1)}, bf16[32,8,512]{2,1,0:T(8,128)(2,1)}, u32[]{:S(2)}) copy-start(bf16[32,8,512]{2,1,0:T(8,128)(2,1)} %param.15) | copy-start | bytes 786436
  152.1 23.4 %all-to-all-start.1 = ((bf16[32,2,8]{2,1,0:T(2,128)(2,1)}), bf16[32,2,8]{2,1,0:T(2,128)(2,1)S(1)}, u32[]{:S(2)}, u32[]{:S(2)}) async-start(bf16[32,2,8]{2,1,0:T(2,128)(2,1)} %bitcast.12), calls=%async_computation.1 | async-start | bytes 32768 | tf_op jit(solution)/shard_map/all_to_all | solution.py:128
  163.8 239.1 %all-reduce.8.cloned.1.call-start = ((), (), s32[]{:S(2)}) async-start(), calls=%async_computation.8 | async-start | bytes 393216 | tf_op jit(solution)/shard_map/psum | solution.py:44
  276.3 59.8 %copy-start.3 = (f32[512]{0:T(512)S(1)}, f32[512]{0:T(512)}, u32[]{:S(2)}) copy-start(f32[512]{0:T(512)} %param.18) | copy-start | bytes 6148
  349.1 374.7 %all-reduce.10.cloned.1.call-start = ((), (), s32[]{:S(2)}) async-start(), calls=%async_computation.10 | async-start | bytes 196608 | tf_op jit(solution)/shard_map/psum | solution.py:184
  402.9 5.0 copy-start.1
  407.9 465.1 %reduce-scatter.2.cloned.1.call-start = ((), (), s32[]{:S(2)}) async-start(), calls=%async_computation.9 | async-start | bytes 4325376 | tf_op jit(solution)/shard_map/reduce_scatter | solution.py:176
  518.5 356.1 %copy-start.6 = (f32[8,32]{1,0:T(8,128)}, f32[8,32]{1,0:T(8,128)S(1)}, u32[]{:S(2)}) copy-start(f32[8,32]{1,0:T(8,128)S(1)} %get-tuple-element.250) | copy-start | bytes 3076
Sparse Core Ops, SparseCore 0:
  60.9 84.5 all-gather.10
  147.6 28.6 all-gather.6
  179.7 92.0 all-gather.8
  273.7 49.9 all-gather.12
  349.3 53.6 all-reduce.7
  408.0 315.8 all-reduce.9
  729.3 143.7 reduce-scatter.1
where the time goes:
time: 887 us; the launch traced here: 883 us
  waiting for transfers between devices  604 us (68%)
  blocking collectives  199 us (22%)
  matrix products  31.7 us (4%)
  between operations  17.6 us (2%)
  starting transfers between devices  12 us (1%)
  local copies, waits for them, and re-layouts  9.84 us (1%)
    psum x1, waiting for transfers between devices, per_device(): lax.psum((policy_grad, value_grad, gain_grad), 'dp')  205 us
    reduce_scatter x1, waiting for transfers between devices, per_device(): lax.psum_scatter(lax.dot_general(learn_context, grad_stream, (((0,), (0,)...  149 us
    psum x1, blocking collectives, per_device(): lax.psum((policy_grad, value_grad, gain_grad), 'dp')  90 us
    all_gather x1, waiting for transfers between devices, per_device(): weights = lax.all_gather(w_out, 'dp', axis=0, tiled=True)  85 us
    psum x1, waiting for transfers between devices, forward(): lax.psum((jnp.dot(normed, policy, precision=highest), jnp.dot(normed, val...  52.9 us
    all_gather x1, waiting for transfers between devices, per_device(): lax.all_gather(got_bulk, 'role', axis=0, tiled=True)  50.9 us
    all_to_all x1, blocking collectives, per_device(): lax.all_to_all(send_bulk, 'dp', split_axis=0, concat_axis=0, tiled=True)  47.5 us
    all_gather x2, waiting for transfers between devices, forward(): context_full = lax.all_gather(context_cols, 'mp', axis=2, tiled=True)  47.4 us
  transfers between devices with their start and end apart: 8, of which 7 were waited for; matrix products, arithmetic and copies ran while one was open for 3% of the time, Pallas kernels for 0%

commit v1 on v0

v1 whole, which is shorter than its diff:
```python
import jax
import jax.numpy as jnp
from jax import lax
from jax.sharding import PartitionSpec as P

D = 2048


discount = 0.99
trace_decay = 0.95
value_weight = 0.5
epsilon = 1e-05
highest = lax.Precision.HIGHEST


def advantage_estimate(rewards, resets, values, lengths):
    num_env, num_steps = values.shape
    valid = (jnp.arange(num_steps)[None, :] < lengths[:, None]).astype(jnp.float32)
    next_values = jnp.concatenate([values[:, 1:], jnp.zeros((num_env, 1), jnp.float32)], axis=1)
    carry_on = 1.0 - resets.astype(jnp.float32)
    deltas = rewards.astype(jnp.float32) + discount * carry_on * next_values - values

    def step_back(later, inputs):
        delta_now, keep_now, valid_now = inputs
        current = valid_now * (delta_now + discount * trace_decay * keep_now * later)
        return (current, current)

    final_carry, stacked = lax.scan(
        step_back, jnp.zeros((num_env,), jnp.float32), (deltas.T, carry_on.T, valid.T), reverse=True
    )
    return (stacked.T, valid)


def per_device(
    residual_in,
    context,
    w_out,
    norm_gain,
    policy_head,
    value_head,
    rewards,
    resets,
    actions,
    lengths,
    assignment,
):
    num_env, num_steps, width_cols = context.shape
    rows = num_env * num_steps
    learners = lax.axis_size("dp")
    num_actions = policy_head.shape[1]
    weights = lax.all_gather(w_out, "dp", axis=0, tiled=True)
    context_full = lax.all_gather(context, "mp", axis=2, tiled=True).reshape(rows, -1)
    heads = jnp.concatenate([policy_head, value_head[:, None]], axis=1).astype(jnp.float32)
    stream = residual_in.reshape(rows, width_cols).astype(jnp.float32) + jnp.dot(
        context_full, weights, preferred_element_type=jnp.float32
    )
    scaled = stream * norm_gain
    raw, squares = lax.psum(
        (jnp.dot(scaled, heads, precision=highest), jnp.sum(stream * stream, axis=1)), "mp"
    )
    inverse = lax.rsqrt(squares / D + epsilon)
    out = raw * inverse[:, None]
    logits, values = out[:, :num_actions], out[:, num_actions]
    value_grid = values.reshape(num_env, num_steps)
    advantages, valid = advantage_estimate(rewards, resets, value_grid, lengths)
    returns = advantages + value_grid
    target_hit = (assignment[:, None] == jnp.arange(learners)[None, :]).astype(jnp.float32)
    both = jnp.stack([lengths.astype(jnp.float32), jnp.sum(advantages, axis=1)])
    totals = lax.psum(jnp.dot(both, target_hit, precision=highest), ("role", "dp"))
    counts, means = totals[0], totals[1] / totals[0]
    env_count = jnp.dot(target_hit, counts, precision=highest)
    env_mean = jnp.dot(target_hit, means, precision=highest)
    centered = (advantages - env_mean[:, None]).reshape(-1)
    weight = (valid / env_count[:, None]).reshape(-1)
    log_probs = logits - jnp.log(jnp.sum(jnp.exp(logits), axis=1, keepdims=True))
    chosen = (actions.reshape(-1)[:, None] == jnp.arange(num_actions)[None, :]).astype(jnp.float32)
    grad_logits = (weight * centered)[:, None] * (jnp.exp(log_probs) - chosen)
    grad_values = value_weight * weight * (values - returns.reshape(-1))
    grad_out = jnp.concatenate([grad_logits, grad_values[:, None]], axis=1)
    grad_normed = jnp.dot(grad_out, heads.T, precision=highest)
    grad_heads = jnp.dot((scaled * inverse[:, None]).T, grad_out, precision=highest)
    gain_grad = jnp.sum(grad_normed * stream * inverse[:, None], axis=0)
    inner = jnp.sum(grad_out * raw, axis=1)
    grad_stream = (
        inverse[:, None] * norm_gain * grad_normed
        - stream * (inverse * inverse * inverse * inner / D)[:, None]
    ).astype(jnp.bfloat16)
    grad_w = lax.psum_scatter(
        lax.dot_general(
            context_full, grad_stream, (((0,), (0,)), ((), ())), preferred_element_type=jnp.float32
        ),
        "dp",
        scatter_dimension=0,
        tiled=True,
    )
    grad_w = lax.psum(grad_w, "role")
    grad_heads, gain_grad = lax.psum((grad_heads, gain_grad), ("role", "dp"))
    adv_means = lax.dynamic_slice(means, (lax.axis_index("dp"),), (1,))
    return (
        advantages,
        adv_means,
        grad_w,
        gain_grad,
        grad_heads[:, :num_actions],
        grad_heads[:, num_actions],
    )


def solution(mesh):
    placed = (
        P(("role", "dp"), None, "mp"),
        P(("role", "dp"), None, "mp"),
        P("dp", "mp"),
        P("mp"),
        P("mp", None),
        P("mp"),
        P(("role", "dp"), None),
        P(("role", "dp"), None),
        P(("role", "dp"), None),
        P(("role", "dp")),
        P(("role", "dp")),
    )
    return jax.shard_map(
        per_device,
        mesh=mesh,
        in_specs=placed,
        out_specs=(
            P(("role", "dp"), None),
            P("dp"),
            P("dp", "mp"),
            P("mp"),
            P("mp", None),
            P("mp"),
        ),
        check_vma=False,
    )
```

time: 887 us -> 991 us (1.12)
  the two profiles are of different devices: /device:TPU:1 before, /device:TPU:258 now
where the time goes in v1:
time: 991 us
  blocking collectives  682 us (69%)
  waiting for transfers between devices  270 us (27%)
  local copies, waits for them, and re-layouts  14.6 us (1%)
  between operations  14 us (1%)
    psum x1, blocking collectives, per_device(): grad_heads, gain_grad = lax.psum((grad_heads, gain_grad), ('role', 'dp'))  334 us
    psum x1, blocking collectives, per_device(): lax.psum(jnp.dot(both, target_hit, precision=highest), ('role', 'dp'))  333 us
    unnamed x6, waiting for transfers between devices  150 us
    all_gather x1, waiting for transfers between devices, per_device(): weights = lax.all_gather(w_out, 'dp', axis=0, tiled=True)  91.8 us
    all_gather x1, waiting for transfers between devices, per_device(): lax.all_gather(context, 'mp', axis=2, tiled=True).reshape(rows, -1)  28.7 us
  transfers between devices with their start and end apart: 5, of which 3 were waited for; matrix products, arithmetic and copies ran while one was open for 1% of the time, Pallas kernels for 0%

profile of v1, /device:TPU:258, one launch (start us, length us, event | category | flops | bytes accessed | tf_op | source)
XLA Modules:
  0.0 990.8 jit_solution(8111119783874562671)
XLA Ops:
  7.2 0.7 all-gather.3.cloned.1.call-update
  8.0 0.7 all-gather.5.cloned.1.call-update
  8.7 0.7 broadcast_in_dim.18
  9.4 0.8 copy.42
  10.3 0.7 convert_bitcast_fusion
  10.9 0.7 fusion.27
  11.6 28.7 %all-gather.3.cloned.1.call-done = bf16[32,8,2048]{2,1,0:T(8,128)(2,1)} async-done(((bf16[32,8,512]{2,1,0:T(8,128)(2,1)}), bf16[32,8,2048]{2,1,0:T(8,128)(2,1)}) %all-gather.3.cloned.1.call-update) | async-done | bytes 1048592 | tf_op jit(solution)/shard_map/all_gather | solution.py:52
  40.3 91.8 %all-gather.5.cloned.1.call-done = bf16[2048,512]{1,0:T(8,128)(2,1)} async-done(((bf16[64,512]{1,0:T(8,128)(2,1)}), bf16[2048,512]{1,0:T(8,128)(2,1)}) %all-gather.5.cloned.1.call-update) | async-done | bytes 2097168 | tf_op jit(solution)/shard_map/all_gather | solution.py:51
  132.1 2.7 multiply_reduce_fusion.1
  134.8 0.4 fusion.12
  135.2 14.5 %all-reduce.1 = (f32[256,44]{0,1:T(8,128)S(1)}, f32[256]{0:T(256)S(1)}) all-reduce(f32[256,44]{0,1:T(8,128)S(1)} %fusion.12, f32[256]{0:T(256)S(1)} %get-tuple-element.205), channel_id=1, replica_groups=mesh['role'=4,'dp'=32,'mp'=4] {'mp'}, use_global_device_ids=true, to_apply=%region_0.0 | all-reduce | flops 11520 | bytes 92160 | tf_op jit(solution)/shard_map/psum | solution.py:58
  150.0 0.6 while.17
  150.8 333.1 %psum.44 = f32[2,32]{1,0:T(2,128)S(1)} all-reduce(f32[2,32]{1,0:T(2,128)S(1)} %fusion.22), channel_id=1, replica_groups=mesh['role'=4,'dp'=32,'mp'=4] {'role','dp'}, use_global_device_ids=true, to_apply=%region_6.7 | all-reduce | flops 64 | bytes 512 | tf_op jit(solution)/shard_map/psum | solution.py:69
  484.9 0.5 multiply_reduce_fusion
  485.4 2.9 convolution_bitcast_fusion
  488.2 5.3 copy.46
  493.6 1.2 fusion.9
  494.9 148.5 %reduce-scatter.4.cloned.1.call-done = f32[64,512]{1,0:T(8,128)} async-done(((f32[2048,512]{1,0:T(8,128)}), f32[64,512]{1,0:T(8,128)}) %reduce-scatter.4.cloned.1.call-update) | async-done | bytes 131088
  643.4 1.7 copy.47
  645.2 0.6 dynamic_slice.31
  645.8 334.0 %psum.46 = f32[512]{0:T(512)} all-reduce(f32[512]{0:T(512)S(1)} %get-tuple-element.207), channel_id=1, replica_groups=mesh['role'=4,'dp'=32,'mp'=4] {'role','dp'}, use_global_device_ids=true, to_apply=%region_12.13 | all-reduce | flops 512 | bytes 4096 | tf_op jit(solution)/shard_map/psum | solution.py:97
  979.8 1.3 slice.32
  981.1 1.7 copy.44
  982.8 1.5 copy.60
  (68 shorter events, 2.2 us)
Async XLA Ops:
  7.2 33.1 %all-gather.3.cloned.1.call-start = ((), (), s32[]{:S(2)}) async-start(), calls=%async_computation.1 | async-start | bytes 1310720 | tf_op jit(solution)/shard_map/all_gather | solution.py:52
  7.9 126.9 %copy-start.1 = (bf16[512,43]{0,1:T(8,128)(2,1)S(1)}, bf16[512,43]{0,1:T(8,128)(2,1)}, u32[]{:S(2)}) copy-start(bf16[512,43]{0,1:T(8,128)(2,1)} %param.17) | copy-start | bytes 132100
  7.9 126.9 %copy-start.2 = (f32[512]{0:T(512)S(1)}, f32[512]{0:T(512)}, u32[]{:S(2)}) copy-start(f32[512]{0:T(512)} %param.16) | copy-start | bytes 6148
  7.9 124.1 %all-gather.5.cloned.1.call-start = ((), (), s32[]{:S(2)}) async-start(), calls=%async_computation.2 | async-start | bytes 2162688 | tf_op jit(solution)/shard_map/all_gather | solution.py:51
  8.7 634.8 %reduce-scatter.4.cloned.1.call-start = ((), (), s32[]{:S(2)}) async-start(), calls=%async_computation.5 | async-start | bytes 4325376
  11.6 138.4 %copy-start.4 = (s32[32,8]{0,1:T(8,128)S(1)}, s32[32,8]{0,1:T(8,128)}, u32[]{:S(2)}) copy-start(s32[32,8]{0,1:T(8,128)} %param.20) | copy-start | bytes 3076
  11.6 138.4 %copy-start.6 = (bf16[32,8]{0,1:T(8,128)(2,1)S(1)}, bf16[32,8]{0,1:T(8,128)(2,1)}, u32[]{:S(2)}) copy-start(bf16[32,8]{0,1:T(8,128)(2,1)} %param.19) | copy-start | bytes 1540
  11.6 139.1 %copy-start.7 = (s32[32]{0:T(128)S(1)}, s32[32]{0:T(128)}, u32[]{:S(2)}) copy-start(s32[32]{0:T(128)} %param.23) | copy-start | bytes 388
  11.6 472.8 %copy-start.5 = (s32[32]{0:T(128)S(1)}, s32[32]{0:T(128)}, u32[]{:S(2)}) copy-start(s32[32]{0:T(128)} %param.22) | copy-start | bytes 388
  134.8 350.6 %copy-start = (bf16[32,8,2048]{2,1,0:T(8,128)(2,1)S(1)}, bf16[32,8,2048]{2,1,0:T(8,128)(2,1)}, u32[]{:S(2)}) copy-start(bf16[32,8,2048]{2,1,0:T(8,128)(2,1)} %all-gather.3.cloned.1.call-done) | copy-start | bytes 3145732
  150.6 337.6 %copy-start.3 = (f32[8,32]{1,0:T(8,128)}, f32[8,32]{1,0:T(8,128)S(1)}, u32[]{:S(2)}) copy-start(f32[8,32]{1,0:T(8,128)S(1)} %get-tuple-element.128) | copy-start | bytes 3076
  493.6 486.2 %all-reduce.7.cloned.1.call-start = ((), (), s32[]{:S(2)}) async-start(), calls=%async_computation.4 | async-start | bytes 196608 | tf_op jit(solution)/shard_map/psum | solution.py:97
  494.9 486.2 %all-reduce.5.cloned.1.call-start = ((), (), s32[]{:S(2)}) async-start(), calls=%async_computation.3 | async-start | bytes 524288 | tf_op jit(solution)/shard_map/psum | solution.py:96
Sparse Core Ops, SparseCore 0:
  10.1 30.1 all-gather.2
  43.6 88.3 all-gather.4
  493.7 149.6 reduce-scatter.3
  647.5 175.4 all-reduce.6
  826.0 52.0 all-reduce.4

commit v2 on v1

v2 whole, which is shorter than its diff:
```python
import jax
import jax.numpy as jnp
from jax import lax
from jax.experimental import pallas as pl
from jax.experimental.pallas import tpu as pltpu
from jax.sharding import PartitionSpec as P

D = 2048
A = 43
STEPS = 8
ROWS = 256
COLS = 512
HALF = 256
HP = 64
RAW = 48

discount = 0.99
trace_decay = 0.95
value_weight = 0.5
epsilon = 1e-05

MESH = pl.DeviceIdType.MESH
bf16 = jnp.bfloat16
f32 = jnp.float32
i32 = jnp.int32

NN = (((1,), (0,)), ((), ()))
NT = (((1,), (1,)), ((), ()))
TN = (((0,), (0,)), ((), ()))


def mul(a, b, dims):
    return lax.dot_general(a, b, dims, preferred_element_type=f32)


def parts_of(a, n):
    out = []
    for _ in range(n):
        high = a.astype(bf16)
        out.append(high)
        a = a - high.astype(f32)
    return out


def kernel(
    resid, ctx, w, gain, policy, value, rewards, resets, actions, lengths, assign,
    adv_out, misc_out, gw_out, heads_out,
    ctxbuf, wa, wb, wm, psend, precv, stream_s, gstream,
    rawbuf, l1, l2, lsrc, heads_t, qsrc, q1, q2, q2src, qf,
    pb, ra, rb, sa2, sb2, ra2, rb2, fin,
    s_ctx, r_ctx, s_a1, r_a1, s_a2, r_a2, s_b1, r_b1, s_b2, r_b2,
    s_p, r_p, s_raw, r_raw, s_l1, r_l1, s_l2, r_l2, s_g, r_g,
    s_q1, r_q1, s_q2, r_q2, s_q3, r_q3,
    s_ra, r_ra, s_rb, r_rb, s_ra2, r_ra2, s_rb2, r_rb2, s_f, r_f,
):
    role = lax.axis_index("role")
    dp = lax.axis_index("dp")
    x = lax.axis_index("mp")
    z = dp // 4
    h = (dp // 2) % 2
    c = dp % 2
    y = h * 4 + role
    r = role
    o = 1 - c
    kx = x // 2
    kz = z // 4
    me16 = z * 2 + c

    def dev(dx, dy, dz, core):
        yy = (y + dy) % 8
        return {
            "role": yy % 4,
            "dp": ((z + dz) % 8) * 4 + (yy // 4) * 2 + core,
            "mp": (x + dx) % 4,
        }

    mate = dev(0, 0, 0, o)

    def remote(src, dst, send, recv, device):
        return pltpu.make_async_remote_copy(
            src_ref=src,
            dst_ref=dst,
            send_sem=send,
            recv_sem=recv,
            device_id=device,
            device_id_type=MESH,
        )

    pending = []

    def send(src, dst, ssem, rsem, device):
        copy = remote(src, dst, ssem, rsem, device)
        copy.start()
        pending.append((None, copy))

    def send_chip(src, dst, ssem, rsem, core):
        @pl.when(c == core)
        def _():
            pltpu.make_async_copy(src, dst, rsem).start()

        copy = remote(src, dst, ssem, rsem, mate)

        @pl.when(c != core)
        def _():
            copy.start()

        pending.append((c != core, copy))

    def arrived(dst, rsem):
        pltpu.make_async_copy(dst, dst, rsem).wait()

    barrier = pltpu.get_barrier_semaphore()
    peers = [mate]
    for d in range(1, 4):
        peers += [dev(d, 0, 0, 0), dev(d, 0, 0, 1)]
    for d in range(1, 8):
        peers += [dev(0, 0, d, 0), dev(0, 0, d, 1), dev(0, d, 0, c)]
    for peer in peers:
        pl.semaphore_signal(barrier, inc=1, device_id=peer, device_id_type=MESH)
    pl.semaphore_wait(barrier, len(peers))

    slot = (x % 2) * 2 + c
    for d in (2, 1, 3):
        send(ctx, ctxbuf.at[slot], s_ctx.at[d], r_ctx.at[slot], dev(d, 0, 0, kx))
    send_chip(ctx, ctxbuf.at[slot], s_ctx.at[0], r_ctx.at[slot], kx)
    zs = z % 4
    quarter = w.at[pl.ds(pl.multiple_of(r * 16, 16), 16), pl.ds(0, HALF)]
    second = w.at[:, pl.ds(HALF, HALF)]
    mirror = {"role": (7 - y) % 4, "dp": z * 4 + (1 - h) * 2 + c, "mp": x}
    send(second, wm, s_b1.at[0], r_b1.at[0], mirror)
    for d in (4, 3, 5, 2, 6, 1, 7):
        send(quarter, wa.at[zs, h, c, r], s_a1.at[d], r_a1.at[zs * 2 + c], dev(0, 0, d, kz))
    send_chip(quarter, wa.at[zs, h, c, r], s_a1.at[0], r_a1.at[zs * 2 + c], kz)
    bslot = (zs * 2 + h) * 2 + c
    for d in (4, 3, 5, 2, 6, 1, 7):
        send(second, wb.at[bslot], s_b2.at[d], r_b2.at[bslot], dev(0, 0, d, kz))
    send_chip(second, wb.at[bslot], s_b2.at[0], r_b2.at[bslot], kz)

    lane8 = lax.broadcasted_iota(i32, (8, ROWS), 1)
    sub8 = lax.broadcasted_iota(i32, (8, ROWS), 0)
    step = lane8 % STEPS
    spread = (step == sub8).astype(f32).astype(bf16)
    lane32 = lax.broadcasted_iota(i32, (32, ROWS), 1)
    sub32 = lax.broadcasted_iota(i32, (32, ROWS), 0)
    env = lane32 // STEPS == sub32
    env_b = env.astype(f32).astype(bf16)

    def to_row(grid):
        wide = jnp.where(env, mul(grid.astype(f32).astype(bf16), spread, NN), 0.0)
        return jnp.broadcast_to(jnp.sum(wide, axis=0, keepdims=True), (8, ROWS))

    def env_row(vector):
        return mul(jnp.broadcast_to(vector.astype(f32), (8, 32)).astype(bf16), env_b, NN)

    reward = to_row(rewards[...])
    keep = 1.0 - to_row(resets[...])
    action = to_row(actions[...])
    length = env_row(lengths[...])
    learner = env_row(assign[...])
    valid = (step.astype(f32) < length).astype(f32)
    learner_hit = jnp.broadcast_to(learner[0:1], (32, ROWS)) == sub32.astype(f32)
    pick = (
        lax.broadcasted_iota(i32, (HP, A), 0) == lax.broadcasted_iota(i32, (HP, A), 1)
    ).astype(f32).astype(bf16)
    head_rows = lax.broadcasted_iota(i32, (HP, COLS), 0)
    heads_t[...] = jnp.where(
        head_rows == A,
        jnp.broadcast_to(value[...].astype(f32), (HP, COLS)),
        mul(pick, policy[...], NT),
    ).astype(bf16)

    arrived(wm, r_b1.at[0])
    cslot = (zs * 2 + 1 - h) * 2 + c
    for d in (4, 3, 5, 2, 6, 1, 7):
        send(wm, wb.at[cslot], s_b2.at[8 + d], r_b2.at[cslot], dev(0, 0, d, kz))
    send_chip(wm, wb.at[cslot], s_b2.at[8], r_b2.at[cslot], kz)
    for s in range(4):
        for core in range(2):
            arrived(wa.at[s, h, core, r], r_a1.at[s * 2 + core])
    mine = wa.at[:, h, :, r]
    for d in (4, 3, 5, 2, 6, 1, 7):
        send(mine, mine, s_a2.at[d], r_a2.at[y], dev(0, d, 0, c))
    for s in range(4):
        arrived(ctxbuf.at[s], r_ctx.at[s])
    for s in range(16):
        arrived(wb.at[s], r_b2.at[s])
    for d in range(1, 8):
        yy = (y + d) % 8
        arrived(wa.at[:, yy // 4, :, yy % 4], r_a2.at[yy])

    def project(core, half):
        buf = wa if half == 0 else wb
        total = None
        for s in range(2):
            if half == 0:
                block = buf[2 * s : 2 * s + 2].reshape(COLS, HALF)
            else:
                block = buf[8 * s : 8 * s + 8].reshape(COLS, HALF)
            term = mul(ctxbuf[2 * s + core], block, NN)
            total = term if total is None else total + term
        return total

    psend[:, 0:HALF] = project(o, 0)
    psend[:, HALF:] = project(o, 1)
    send(psend, precv, s_p.at[0], r_p.at[0], mate)
    stream_s[:, 0:HALF] = resid[:, 0:HALF].astype(f32) + project(c, 0)
    stream_s[:, HALF:] = resid[:, HALF:].astype(f32) + project(c, 1)
    arrived(precv, r_p.at[0])
    stream = stream_s[...] + precv[...]
    stream_s[...] = stream

    gains = gain[...]
    raw = None
    for part in parts_of(stream * gains, 3):
        term = mul(heads_t[...], part, NT)
        raw = term if raw is None else raw + term
    square = None
    for part in parts_of(stream * stream, 3):
        term = mul(jnp.ones((16, COLS), bf16), part, NT)
        square = term if square is None else square + term
    raw_rows = lax.broadcasted_iota(i32, (RAW, ROWS), 0)
    rawbuf[x] = jnp.where(
        raw_rows == A + 1, jnp.broadcast_to(square[0:1], (RAW, ROWS)), raw[0:RAW]
    )
    for d in (2, 1, 3):
        send(rawbuf.at[x], rawbuf.at[x], s_raw.at[d], r_raw.at[x], dev(d, 0, 0, c))
    for d in (1, 3, 2):
        xx = (x + d) % 4
        arrived(rawbuf.at[xx], r_raw.at[xx])
    raw = ((rawbuf[0] + rawbuf[1]) + rawbuf[2]) + rawbuf[3]

    inverse = lax.rsqrt(jnp.broadcast_to(raw[A + 1 : A + 2], (8, ROWS)) / D + epsilon)
    out = raw * jnp.broadcast_to(inverse[0:1], (RAW, ROWS))
    values = jnp.broadcast_to(out[A : A + 1], (8, ROWS))

    def later(v, n):
        return pltpu.roll(v, ROWS - n, 1)

    last = step == STEPS - 1
    next_values = jnp.where(last, 0.0, later(values, 1))
    delta = reward + discount * keep * next_values - values
    adv = valid * delta
    factor = jnp.where(last, 0.0, valid * (discount * trace_decay) * keep)
    adv = adv + factor * later(adv, 1)
    factor = factor * later(factor, 1)
    adv = adv + factor * later(adv, 2)
    factor = factor * later(factor, 2)
    adv = adv + factor * later(adv, 4)

    adv32 = jnp.broadcast_to(adv[0:1], (32, ROWS))
    valid32 = jnp.broadcast_to(valid[0:1], (32, ROWS))
    sums = jnp.sum(jnp.where(learner_hit, adv32, 0.0), axis=1, keepdims=True)
    counts = jnp.sum(jnp.where(learner_hit, valid32, 0.0), axis=1, keepdims=True)
    lane128 = lax.broadcasted_iota(i32, (32, 128), 1)
    sub128 = lax.broadcasted_iota(i32, (32, 128), 0)
    at_sum = lane128 == sub128
    at_count = lane128 == sub128 + 32
    message = jnp.sum(
        jnp.where(at_sum, sums, 0.0) + jnp.where(at_count, counts, 0.0), axis=0, keepdims=True
    )
    l1[me16] = message
    lsrc[...] = message
    for d in (4, 3, 5, 2, 6, 1, 7):
        for core in range(2):
            send(lsrc, l1.at[me16], s_l1.at[2 * d + core], r_l1.at[me16], dev(0, 0, d, core))
    send(lsrc, l1.at[me16], s_l1.at[0], r_l1.at[me16], mate)

    act_rows = raw_rows < A
    logits = jnp.where(act_rows, out, -1e30)
    top = jnp.max(logits, axis=0, keepdims=True)
    expo = jnp.where(act_rows, jnp.exp(logits - top), 0.0)
    prob = expo / jnp.sum(expo, axis=0, keepdims=True)
    chosen = raw_rows.astype(f32) == jnp.broadcast_to(action[0:1], (RAW, ROWS))
    score = prob - jnp.where(chosen, 1.0, 0.0)

    for s in range(1, 16):
        ss = (me16 + s) % 16
        arrived(l1.at[ss], r_l1.at[ss])
    total = l1[0]
    for s in range(1, 16):
        total = total + l1[s]
    l2[y] = total
    for d in (4, 3, 5, 2, 6, 1, 7):
        send(l2.at[y], l2.at[y], s_l2.at[d], r_l2.at[y], dev(0, d, 0, c))
    e8 = jnp.where(env, adv32, 0.0)
    adv_grid = None
    for part in parts_of(e8, 3):
        term = mul(part, spread, NT)
        adv_grid = term if adv_grid is None else adv_grid + term
    adv_out[...] = adv_grid
    for d in range(1, 8):
        yy = (y + d) % 8
        arrived(l2.at[yy], r_l2.at[yy])
    total = l2[0]
    for s in range(1, 8):
        total = total + l2[s]
    wide = jnp.broadcast_to(total, (32, 128))
    sums = jnp.sum(jnp.where(at_sum, wide, 0.0), axis=1, keepdims=True)
    counts = jnp.sum(jnp.where(at_count, wide, 0.0), axis=1, keepdims=True)
    means = sums / counts
    own = jnp.sum(jnp.where(sub128 == dp, means, 0.0), axis=0, keepdims=True)
    misc_out[...] = jnp.broadcast_to(own, (8, 128))

    mean_row = jnp.sum(jnp.where(learner_hit, means, 0.0), axis=0, keepdims=True)
    count_row = jnp.sum(jnp.where(learner_hit, counts, 0.0), axis=0, keepdims=True)
    weight = valid[0:1] / count_row
    centered = adv[0:1] - mean_row
    grad_value_row = -value_weight * weight * adv[0:1]
    grad_out = jnp.where(
        act_rows,
        (weight * centered) * score,
        jnp.where(raw_rows == A, jnp.broadcast_to(grad_value_row, (RAW, ROWS)), 0.0),
    )
    inner = jnp.sum(grad_out * raw, axis=0, keepdims=True)
    inv = inverse[0:1]
    coef = inv * inv * inv * inner / D
    scaled_out = grad_out * inv
    tall = jnp.concatenate(
        [scaled_out, jnp.broadcast_to(coef, (HP - RAW, ROWS))], axis=0
    )
    tall_rows = lax.broadcasted_iota(i32, (HP, ROWS), 0)
    tall = jnp.where(tall_rows <= RAW, tall, 0.0)
    tall_parts = parts_of(tall, 2)

    one_row = (lax.broadcasted_iota(i32, (HP, 128), 0) == RAW).astype(f32).astype(bf16)
    grad_normed = mul(tall_parts[0], heads_t[...], TN) + mul(tall_parts[1], heads_t[...], TN)
    coef_col = mul(tall_parts[0], one_row, TN) + mul(tall_parts[1], one_row, TN)
    stream = stream_s[...]
    coef_wide = jnp.concatenate([coef_col] * 4, axis=1)
    gstream[c] = (gains * grad_normed - stream * coef_wide).astype(bf16)
    send(gstream.at[c], gstream.at[c], s_g.at[0], r_g.at[0], mate)

    high, low = parts_of(stream, 2)
    q = mul(tall_parts[0], high, NN) + mul(tall_parts[0], low, NN) + mul(tall_parts[1], high, NN)
    for p in range(16):
        qsrc[p] = q[(p % 4) * 16 : (p % 4) * 16 + 16, (p // 4) * 128 : (p // 4) * 128 + 128]
    q1[me16] = qsrc[me16]
    for d in (4, 3, 5, 2, 6, 1, 7):
        for core in range(2):
            part = ((z + d) % 8) * 2 + core
            send(qsrc.at[part], q1.at[me16], s_q1.at[2 * d + core], r_q1.at[me16], dev(0, 0, d, core))
    send(qsrc.at[z * 2 + o], q1.at[me16], s_q1.at[0], r_q1.at[me16], mate)

    arrived(gstream.at[o], r_g.at[0])
    for s in range(2):
        block = mul(ctxbuf[2 * s], gstream[0], TN) + mul(ctxbuf[2 * s + 1], gstream[1], TN)
        pb[2 * s : 2 * s + 2] = block.astype(bf16).reshape(2, 2, 2, 4, 16, COLS)
    first_cols, last_cols = pl.ds(0, HALF), pl.ds(HALF, HALF)

    def send_z(src_of, dst, ssem, rsem):
        for s in range(4):
            away = (4 * c + s) != z
            dz = 4 * c + s - z + 8
            for core in range(2):
                copy = remote(src_of(s, core), dst, ssem.at[2 * s + core], rsem, dev(0, 0, dz, core))

                @pl.when(away)
                def _():
                    copy.start()

                pending.append((away, copy))
            own_copy = remote(src_of(s, o), dst, ssem.at[8], rsem, mate)

            @pl.when(jnp.logical_not(away))
            def _():
                pltpu.make_async_copy(src_of(s, c), dst, rsem).start()
                own_copy.start()

            pending.append((jnp.logical_not(away), own_copy))

    send_z(lambda s, core: pb.at[s, :, core, :, :, first_cols], ra.at[z], s_ra, r_ra.at[z])
    for d in (4, 3, 5, 2, 6, 1, 7):
        yy = (y + d) % 8
        send(
            pb.at[:, yy // 4, :, yy % 4, :, last_cols], rb.at[y], s_rb.at[d], r_rb.at[y], dev(0, d, 0, c)
        )
    rb[y] = pb[:, h, :, r, :, HALF:]

    for s in range(1, 16):
        ss = (me16 + s) % 16
        arrived(q1.at[ss], r_q1.at[ss])
    total = q1[0]
    for s in range(1, 16):
        total = total + q1[s]
    q2[y] = total
    for d in (4, 3, 5, 2, 6, 1, 7):
        send(q2.at[y], q2.at[y], s_q2.at[d], r_q2.at[y], dev(0, d, 0, c))
    for d in range(1, 8):
        yy = (y + d) % 8
        arrived(q2.at[yy], r_q2.at[yy])
    total = q2[0]
    for s in range(1, 8):
        total = total + q2[s]
    qf[me16] = total
    q2src[...] = total
    for d in (4, 3, 5, 2, 6, 1, 7):
        for core in range(2):
            send(q2src, qf.at[me16], s_q3.at[2 * d + core], r_q3.at[me16], dev(0, 0, d, core))
    send(q2src, qf.at[me16], s_q3.at[0], r_q3.at[me16], mate)

    for d in range(8):
        zz = (z + d) % 8
        arrived(ra.at[zz], r_ra.at[zz])
    total = ra[0].astype(f32)
    for s in range(1, 8):
        total = total + ra[s].astype(f32)
    sa2[...] = total
    for d in (4, 3, 5, 2, 6, 1, 7):
        yy = (y + d) % 8
        send(sa2.at[yy // 4, yy % 4], ra2.at[y], s_ra2.at[d], r_ra2.at[y], dev(0, d, 0, c))
    ra2[y] = sa2[h, r]
    for d in range(1, 8):
        yy = (y + d) % 8
        arrived(rb.at[yy], r_rb.at[yy])
    total = rb[0].astype(f32)
    for s in range(1, 8):
        total = total + rb[s].astype(f32)
    sb2[...] = total
    send_z(lambda s, core: sb2.at[s, core], rb2.at[z], s_rb2, r_rb2.at[z])
    for d in range(1, 8):
        yy = (y + d) % 8
        arrived(ra2.at[yy], r_ra2.at[yy])
    total = ra2[0]
    for s in range(1, 8):
        total = total + ra2[s]
    fin[r, :, 0:HALF] = total
    for d in range(8):
        zz = (z + d) % 8
        arrived(rb2.at[zz], r_rb2.at[zz])
    total = rb2[0]
    for s in range(1, 8):
        total = total + rb2[s]
    fin[r, :, HALF:] = total
    for d in (2, 1, 3):
        rr = (r + d) % 4
        device = {"role": rr, "dp": dp, "mp": x}
        send(fin.at[r], fin.at[r], s_f.at[d], r_f.at[r], device)

    for s in range(1, 16):
        ss = (me16 + s) % 16
        arrived(qf.at[ss], r_q3.at[ss])
    gain_rows = []
    for lane in range(4):
        cols = slice(lane * 128, lane * 128 + 128)
        block = jnp.concatenate([qf[lane * 4 + s] for s in range(3)], axis=0)
        gain_row = jnp.sum(block * heads_t[0:RAW, cols].astype(f32), axis=0, keepdims=True)
        rows = lax.broadcasted_iota(i32, (RAW, 128), 0)
        heads_out[:, cols] = jnp.where(
            rows == A + 1, jnp.broadcast_to(gain_row, (RAW, 128)), block * gains[:, cols]
        )

    for d in range(1, 4):
        rr = (r + d) % 4
        arrived(fin.at[rr], r_f.at[rr])
    for s in range(4):
        gw_out[16 * s : 16 * s + 16] = fin[s]

    for condition, copy in pending:
        if condition is None:
            copy.wait_send()
        else:
            pl.when(condition)(copy.wait_send)


def per_device(
    residual_in,
    context,
    w_out,
    norm_gain,
    policy_head,
    value_head,
    rewards,
    resets,
    actions,
    lengths,
    assignment,
):
    vmem = pl.BlockSpec(memory_space=pltpu.VMEM)
    dma = pltpu.SemaphoreType.DMA
    buffers = [
        pltpu.VMEM((4, ROWS, COLS), bf16),
        pltpu.VMEM((4, 2, 2, 4, 16, HALF), bf16),
        pltpu.VMEM((16, 64, HALF), bf16),
        pltpu.VMEM((64, HALF), bf16),
        pltpu.VMEM((ROWS, COLS), f32),
        pltpu.VMEM((ROWS, COLS), f32),
        pltpu.VMEM((ROWS, COLS), f32),
        pltpu.VMEM((2, ROWS, COLS), bf16),
        pltpu.VMEM((4, RAW, ROWS), f32),
        pltpu.VMEM((16, 1, 128), f32),
        pltpu.VMEM((8, 1, 128), f32),
        pltpu.VMEM((1, 128), f32),
        pltpu.VMEM((HP, COLS), bf16),
        pltpu.VMEM((16, 16, 128), f32),
        pltpu.VMEM((16, 16, 128), f32),
        pltpu.VMEM((8, 16, 128), f32),
        pltpu.VMEM((16, 128), f32),
        pltpu.VMEM((16, 16, 128), f32),
        pltpu.VMEM((4, 2, 2, 4, 16, COLS), bf16),
        pltpu.VMEM((8, 2, 4, 16, HALF), bf16),
        pltpu.VMEM((8, 4, 2, 16, HALF), bf16),
        pltpu.VMEM((2, 4, 16, HALF), f32),
        pltpu.VMEM((4, 2, 16, HALF), f32),
        pltpu.VMEM((8, 16, HALF), f32),
        pltpu.VMEM((8, 16, HALF), f32),
        pltpu.VMEM((4, 16, COLS), f32),
    ]
    counts = [4, 4, 8, 8, 8, 8, 1, 1, 16, 16, 1, 1, 4, 4, 16, 16, 8, 8, 1, 1]
    counts += [16, 16, 8, 8, 16, 16]
    counts += [9, 8, 8, 8, 8, 8, 9, 8, 4, 4]
    adv, misc, grad_w, heads = pl.pallas_call(
        kernel,
        out_shape=(
            jax.ShapeDtypeStruct((32, STEPS), f32),
            jax.ShapeDtypeStruct((8, 128), f32),
            jax.ShapeDtypeStruct((64, COLS), f32),
            jax.ShapeDtypeStruct((RAW, COLS), f32),
        ),
        in_specs=[vmem] * 11,
        out_specs=(vmem,) * 4,
        scratch_shapes=buffers + [dma((n,)) for n in counts],
        compiler_params=pltpu.CompilerParams(
            collective_id=0, has_side_effects=True, vmem_limit_bytes=48 * 1024 * 1024
        ),
        name="policy_step",
    )(
        residual_in.reshape(ROWS, COLS),
        context.reshape(ROWS, COLS),
        w_out,
        norm_gain.reshape(1, COLS),
        policy_head,
        value_head.reshape(1, COLS),
        rewards,
        resets,
        actions,
        lengths.reshape(1, 32),
        assignment.reshape(1, 32),
    )
    return (adv, misc[0, 0:1], grad_w, heads[A + 1], heads[0:A].T, heads[A])


def solution(mesh):
    placed = (
        P(("role", "dp"), None, "mp"),
        P(("role", "dp"), None, "mp"),
        P("dp", "mp"),
        P("mp"),
        P("mp", None),
        P("mp"),
        P(("role", "dp"), None),
        P(("role", "dp"), None),
        P(("role", "dp"), None),
        P(("role", "dp")),
        P(("role", "dp")),
    )
    return jax.shard_map(
        per_device,
        mesh=mesh,
        in_specs=placed,
        out_specs=(
            P(("role", "dp"), None),
            P("dp"),
            P("dp", "mp"),
            P("mp"),
            P("mp", None),
            P("mp"),
        ),
        check_vma=False,
    )
```

time: 991 us -> 93.8 us (0.09)
  the two profiles are of different devices: /device:TPU:258 before, /device:TPU:1 now
where the time goes in v2:
time: 93.8 us; the launch traced here: 93.4 us
  Pallas kernels  83.9 us (89%)
  local copies, waits for them, and re-layouts  8.77 us (9%)
    pallas_call x1, Pallas kernels, per_device(): pl.pallas_call(kernel, out_shape=(jax.ShapeDtypeStruct((32, STEPS), f32),...  83.9 us
    unnamed x20, local copies, waits for them, and re-layouts  6.33 us

profile of v2, /device:TPU:1, one launch (start us, length us, event | category | flops | bytes accessed | tf_op | source)
XLA Modules:
  0.0 93.4 jit_solution(2948054213739822054)
XLA Ops:
  0.6 0.0 copy-start.6
  0.6 0.7 reshape.33.value
  1.3 0.8 copy.18.rewards
  2.1 0.8 copy.19.resets
  2.9 0.8 copy.20.actions
  3.6 0.0 copy-done.6
  3.6 0.0 copy-start.2
  3.6 0.0 copy-start.3
  3.6 0.0 copy-start.4
  3.6 0.0 copy-start.5
  3.7 0.1 copy.17.policy
  3.8 0.7 copy-done.2
  4.5 0.0 copy-done.3
  4.5 0.0 copy-done.4
  4.5 0.0 copy-done.5
  4.5 0.0 copy-start
  4.5 0.9 %copy-done = bf16[32,8,512]{2,1,0:T(8,128)(2,1)S(1)} copy-done((bf16[32,8,512]{2,1,0:T(8,128)(2,1)S(1)}, bf16[32,8,512]{2,1,0:T(8,128)(2,1)}, u32[]{:S(2)}) %copy-start) | copy-done | bytes 262168
  5.4 0.9 %copy-done.1 = bf16[32,8,512]{2,1,0:T(8,128)(2,1)S(1)} copy-done((bf16[32,8,512]{2,1,0:T(8,128)(2,1)S(1)}, bf16[32,8,512]{2,1,0:T(8,128)(2,1)}, u32[]{:S(2)}) %copy-start.1) | copy-done | bytes 262168
  6.4 83.9 %policy_step.1 = (f32[32,8]{1,0:T(8,128)S(1)}, f32[8,128]{1,0:T(8,128)S(1)}, f32[64,512]{1,0:T(8,128)S(1)}, f32[48,512]{1,0:T(8,128)S(1)}) custom-call(bf16[256,512]{1,0:T(8,128)(2,1)S(1)} %bitcast.10, bf16[256,512]{1,0:T(8,128)(2,1)S(1)} %bitcast.11, bf16[64,512]{1,0:T(8,128)(2,1)S(1)} %copy-done.2, f32[1,512]{1,0:T(1,128)S(1)} %bitcast.12, ...), custom_call_target="tpu_custom_call" | custom-call | tf_op jit(solution)/shard_map/policy_step/pallas_call | solution.py:511
  90.3 0.5 slice.12
  90.8 0.7 copy.21
  91.5 0.6 fusion
  92.1 0.6 slice_bitcast_fusion
  92.7 0.7 copy.23
  (1 shorter events, 0.0 us)
Async XLA Ops:
  0.6 3.0 %copy-start.6 = (bf16[512,43]{0,1:T(8,128)(2,1)S(1)}, bf16[512,43]{0,1:T(8,128)(2,1)}, u32[]{:S(2)}) copy-start(bf16[512,43]{0,1:T(8,128)(2,1)} %param.15) | copy-start | bytes 132100
  3.6 0.8 copy-start.2
  3.6 0.8 copy-start.3
  3.6 0.8 copy-start.4
  3.6 0.8 copy-start.5
  4.5 1.0 %copy-start = (bf16[32,8,512]{2,1,0:T(8,128)(2,1)S(1)}, bf16[32,8,512]{2,1,0:T(8,128)(2,1)}, u32[]{:S(2)}) copy-start(bf16[32,8,512]{2,1,0:T(8,128)(2,1)} %param.11) | copy-start | bytes 786436
  5.4 0.9 %copy-start.1 = (bf16[32,8,512]{2,1,0:T(8,128)(2,1)S(1)}, bf16[32,8,512]{2,1,0:T(8,128)(2,1)}, u32[]{:S(2)}) copy-start(bf16[32,8,512]{2,1,0:T(8,128)(2,1)} %param.12) | copy-start | bytes 786436

commit v3 on v2

v3 whole, which is shorter than its diff:
```python
import jax
import jax.numpy as jnp
from jax import lax
from jax.experimental import pallas as pl
from jax.experimental.pallas import tpu as pltpu
from jax.sharding import PartitionSpec as P

D = 2048
A = 43
STEPS = 8
ROWS = 256
COLS = 512
HALF = 256
HP = 64
RAW = 48

discount = 0.99
trace_decay = 0.95
value_weight = 0.5
epsilon = 1e-05

MESH = pl.DeviceIdType.MESH
bf16 = jnp.bfloat16
f32 = jnp.float32
i32 = jnp.int32

NN = (((1,), (0,)), ((), ()))
NT = (((1,), (1,)), ((), ()))
TN = (((0,), (0,)), ((), ()))


def mul(a, b, dims):
    return lax.dot_general(a, b, dims, preferred_element_type=f32)


def parts_of(a, n):
    out = []
    for _ in range(n):
        high = a.astype(bf16)
        out.append(high)
        a = a - high.astype(f32)
    return out


FAR_FIRST = (4, 3, 5, 2, 6, 1, 7)


def kernel(
    resid_h, ctx_h, w_h, gain_h, policy_h, value_h,
    rewards_h, resets_h, actions_h, lengths_h, assign_h,
    adv_out, misc_out, gw_out, heads_out,
    resid, gain, policy, value, rewards, resets, actions, lengths, assign,
    ctxbuf, ctx_t, wbuf, psend, precv, stream_s, gstream,
    rawbuf, l1, l2, lsrc, heads_t, qsrc, qmate, qsum, q1, q2, qf,
    pb, ra, rb, sa2, sb2, ra2, rb2,
    s_all, r_in, r_ctx, r_w, r_p, r_raw, r_l1, r_l2, r_g,
    r_q0, r_q1, r_q2, r_q3, r_q4, r_ra, r_rb, r_ra2, r_rb2, r_f,
):
    role = lax.axis_index("role")
    dp = lax.axis_index("dp")
    x = lax.axis_index("mp")
    z = dp // 4
    h = (dp // 2) % 2
    c = dp % 2
    y = h * 4 + role
    r = role
    o = 1 - c
    me16 = z * 2 + c

    def dev(dx, dy, dz, core):
        yy = (y + dy + 8) % 8
        return {
            "role": yy % 4,
            "dp": ((z + dz + 8) % 8) * 4 + (yy // 4) * 2 + core,
            "mp": (x + dx + 4) % 4,
        }

    mate = dev(0, 0, 0, o)
    pending = []

    def remote(src, dst, rsem, device):
        slot = len(pending)
        return pltpu.make_async_remote_copy(
            src_ref=src,
            dst_ref=dst,
            send_sem=s_all.at[slot],
            recv_sem=rsem,
            device_id=device,
            device_id_type=MESH,
        )

    def send(src, dst, rsem, device):
        copy = remote(src, dst, rsem, device)
        copy.start()
        pending.append((None, copy))

    def send_or_keep(here, src, dst, rsem, device):
        copy = remote(src, dst, rsem, device)
        away = jnp.logical_not(here)

        @pl.when(here)
        def _():
            pltpu.make_async_copy(src, dst, rsem).start()

        @pl.when(away)
        def _():
            copy.start()

        pending.append((away, copy))

    def arrived(dst, rsem):
        pltpu.make_async_copy(dst, dst, rsem).wait()

    small = [
        (gain_h, gain), (policy_h, policy), (value_h, value), (rewards_h, rewards),
        (resets_h, resets), (actions_h, actions), (lengths_h, lengths), (assign_h, assign),
        (resid_h, resid),
    ]
    for n, (src, dst) in enumerate(small):
        pltpu.make_async_copy(src, dst, r_in.at[n]).start()

    barrier = pltpu.get_barrier_semaphore()
    peers = [mate, dev(1, 0, 0, 0), dev(1, 0, 0, 1), dev(3, 0, 0, 0), dev(3, 0, 0, 1)]
    peers += [dev(0, 0, 1, c), dev(0, 0, 7, c)]
    peers += [dev(0, d, 0, c) for d in range(1, 8)]
    peers += [{"role": 3 - r, "dp": z * 4 + (1 - h) * 2 + o, "mp": x}]
    for peer in peers:
        pl.semaphore_signal(barrier, inc=1, device_id=peer, device_id_type=MESH)
    pl.semaphore_wait(barrier, len(peers))

    send_or_keep(c == h, w_h, wbuf.at[z, c], r_w.at[z * 2 + c], mate)
    mirror = {"role": 3 - r, "dp": z * 4 + (1 - h) * 2 + h, "mp": x}
    send(w_h, wbuf.at[z, c], r_w.at[z * 2 + c], mirror)

    def piece(zz, core):
        return ctx_h.at[:, pl.ds(pl.multiple_of(zz * 256 + core * 128, 128), 128)]

    def ctx_sem(m, cc, zz):
        return r_ctx.at[(m * 2 + cc) * 2 + zz]

    for first in range(2):
        for dx, zz in ((1, first), (3, 1 - first)):
            for core in range(2):
                send(piece(zz, core), ctxbuf.at[x, c, zz], ctx_sem(x, c, zz), dev(dx, 0, 0, core))
    for zz in range(2):
        pltpu.make_async_copy(piece(zz, c), ctxbuf.at[x, c, zz], ctx_sem(x, c, zz)).start()
        send(piece(zz, o), ctxbuf.at[x, c, zz], ctx_sem(x, c, zz), mate)

    up, down = dev(0, 0, 1, c), dev(0, 0, 7, c)

    def w_block(zz, cc):
        return wbuf.at[zz, cc], r_w.at[zz * 2 + cc]

    for cc in range(2):
        block, sem = w_block(z, cc)
        arrived(block, sem)
        send(block, block, sem, up)
        send(block, block, sem, down)

    for n in range(9):
        pltpu.make_async_copy(small[n][0], small[n][1], r_in.at[n]).wait()
    lane8 = lax.broadcasted_iota(i32, (8, ROWS), 1)
    sub8 = lax.broadcasted_iota(i32, (8, ROWS), 0)
    step = lane8 % STEPS
    own_step = step == sub8
    lane32 = lax.broadcasted_iota(i32, (32, ROWS), 1)
    sub32 = lax.broadcasted_iota(i32, (32, ROWS), 0)
    env_b = (lane32 // STEPS == sub32).astype(f32).astype(bf16)

    def to_row(grid):
        wide = jnp.where(own_step, mul(grid.astype(f32).astype(bf16), env_b, NN), 0.0)
        return jnp.broadcast_to(jnp.sum(wide, axis=0, keepdims=True), (8, ROWS))

    def env_row(vector):
        return mul(jnp.broadcast_to(vector.astype(f32), (8, 32)).astype(bf16), env_b, NN)

    reward = to_row(rewards[...])
    keep = 1.0 - to_row(resets[...])
    action = to_row(actions[...])
    length = env_row(lengths[...])
    learner = env_row(assign[...])
    valid = (step.astype(f32) < length).astype(f32)
    learner_hit = jnp.broadcast_to(learner[0:1], (32, ROWS)) == sub32.astype(f32)
    head_rows = lax.broadcasted_iota(i32, (HP, COLS), 0)
    heads_t[...] = jnp.where(
        head_rows == A,
        jnp.broadcast_to(value[...].astype(f32).reshape(1, COLS), (HP, COLS)),
        jnp.concatenate([policy[...].astype(f32), jnp.zeros((HP - A, COLS), f32)], axis=0),
    ).astype(bf16)

    for m, zz, dx in (((x + 3) % 4, 0, 1), ((x + 1) % 4, 1, 3)):
        for cc in range(2):
            block = ctxbuf.at[m, cc, zz]
            arrived(block, ctx_sem(m, cc, zz))
            send(block, block, ctx_sem(m, cc, zz), dev(dx, 0, 0, c))

    for s in range(1, 5):
        for cc in range(2):
            for sign, target, most in ((-1, up, 4 - cc), (1, down, 3 + cc)):
                if s <= most:
                    block, sem = w_block((z + sign * s + 8) % 8, cc)
                    arrived(block, sem)
                    if s < most:
                        send(block, block, sem, target)

    for cc in range(2):
        for zz in range(2):
            arrived(ctxbuf.at[x, cc, zz], ctx_sem(x, cc, zz))
            m = (x + 2) % 4
            arrived(ctxbuf.at[m, cc, zz], ctx_sem(m, cc, zz))
        m = (x + 3) % 4
        arrived(ctxbuf.at[m, cc, 1], ctx_sem(m, cc, 1))
        m = (x + 1) % 4
        arrived(ctxbuf.at[m, cc, 0], ctx_sem(m, cc, 0))

    def project(core):
        total = None
        for m in range(4):
            left = jnp.concatenate([ctxbuf[m, core, 0], ctxbuf[m, core, 1]], axis=1)
            term = mul(left, wbuf[2 * m : 2 * m + 2].reshape(256, COLS), NN)
            total = term if total is None else total + term
        return total

    psend[...] = project(o)
    send(psend, precv, r_p.at[0], mate)
    stream_s[...] = resid[...].astype(f32) + project(c)
    arrived(precv, r_p.at[0])
    stream = stream_s[...] + precv[...]
    stream_s[...] = stream

    gains = gain[...]
    raw = None
    for part in parts_of(stream * gains, 3):
        term = mul(heads_t[...], part, NT)
        raw = term if raw is None else raw + term
    square = None
    for part in parts_of(stream * stream, 3):
        term = mul(jnp.ones((16, COLS), bf16), part, NT)
        square = term if square is None else square + term
    raw_rows = lax.broadcasted_iota(i32, (RAW, ROWS), 0)
    rawbuf[x] = jnp.where(
        raw_rows == A + 1, jnp.broadcast_to(square[0:1], (RAW, ROWS)), raw[0:RAW]
    )
    for d in (2, 1, 3):
        send(rawbuf.at[x], rawbuf.at[x], r_raw.at[x], dev(d, 0, 0, c))
    for m in range(4):
        for zz in range(2):
            for cc in range(2):
                ctx_t[2 * m + zz, :, cc * ROWS : cc * ROWS + ROWS] = ctxbuf[m, cc, zz].T
    for d in (1, 3, 2):
        xx = (x + d) % 4
        arrived(rawbuf.at[xx], r_raw.at[xx])
    raw = ((rawbuf[0] + rawbuf[1]) + rawbuf[2]) + rawbuf[3]

    inverse = lax.rsqrt(jnp.broadcast_to(raw[A + 1 : A + 2], (8, ROWS)) / D + epsilon)
    out = raw * jnp.broadcast_to(inverse[0:1], (RAW, ROWS))
    values = jnp.broadcast_to(out[A : A + 1], (8, ROWS))

    def later(v, n):
        return pltpu.roll(v, ROWS - n, 1)

    last = step == STEPS - 1
    next_values = jnp.where(last, 0.0, later(values, 1))
    delta = reward + discount * keep * next_values - values
    adv = valid * delta
    factor = jnp.where(last, 0.0, valid * (discount * trace_decay) * keep)
    adv = adv + factor * later(adv, 1)
    factor = factor * later(factor, 1)
    adv = adv + factor * later(adv, 2)
    factor = factor * later(factor, 2)
    adv = adv + factor * later(adv, 4)

    adv32 = jnp.broadcast_to(adv[0:1], (32, ROWS))
    valid32 = jnp.broadcast_to(valid[0:1], (32, ROWS))
    sums = jnp.sum(jnp.where(learner_hit, adv32, 0.0), axis=1, keepdims=True)
    counts = jnp.sum(jnp.where(learner_hit, valid32, 0.0), axis=1, keepdims=True)
    lane128 = lax.broadcasted_iota(i32, (32, 128), 1)
    sub128 = lax.broadcasted_iota(i32, (32, 128), 0)
    at_sum = lane128 == sub128
    at_count = lane128 == sub128 + 32
    message = jnp.sum(
        jnp.where(at_sum, sums, 0.0) + jnp.where(at_count, counts, 0.0), axis=0, keepdims=True
    )
    l1[me16] = message
    lsrc[...] = message
    for d in FAR_FIRST:
        for core in range(2):
            send(lsrc, l1.at[me16], r_l1.at[me16], dev(0, 0, d, core))
    send(lsrc, l1.at[me16], r_l1.at[me16], mate)

    act_rows = raw_rows < A
    logits = jnp.where(act_rows, out, -1e30)
    top = jnp.max(logits, axis=0, keepdims=True)
    expo = jnp.where(act_rows, jnp.exp(logits - top), 0.0)
    prob = expo / jnp.sum(expo, axis=0, keepdims=True)
    chosen = raw_rows.astype(f32) == jnp.broadcast_to(action[0:1], (RAW, ROWS))
    score = prob - jnp.where(chosen, 1.0, 0.0)
    adv_grid = None
    for part in parts_of(jnp.where(own_step, adv, 0.0), 3):
        term = mul(part, env_b, NT)
        adv_grid = term if adv_grid is None else adv_grid + term
    adv_out[...] = adv_grid

    for s in range(1, 16):
        ss = (me16 + s) % 16
        arrived(l1.at[ss], r_l1.at[ss])
    total = l1[0]
    for s in range(1, 16):
        total = total + l1[s]
    l2[y] = total
    for d in FAR_FIRST:
        send(l2.at[y], l2.at[y], r_l2.at[y], dev(0, d, 0, c))
    for d in range(1, 8):
        yy = (y + d) % 8
        arrived(l2.at[yy], r_l2.at[yy])
    total = l2[0]
    for s in range(1, 8):
        total = total + l2[s]
    wide = jnp.broadcast_to(total, (32, 128))
    sums = jnp.sum(jnp.where(at_sum, wide, 0.0), axis=1, keepdims=True)
    counts = jnp.sum(jnp.where(at_count, wide, 0.0), axis=1, keepdims=True)
    means = sums / counts
    own = jnp.sum(jnp.where(sub128 == dp, means, 0.0), axis=0, keepdims=True)
    misc_out[...] = jnp.broadcast_to(own, (8, 128))

    mean_row = jnp.sum(jnp.where(learner_hit, means, 0.0), axis=0, keepdims=True)
    count_row = jnp.sum(jnp.where(learner_hit, counts, 0.0), axis=0, keepdims=True)
    weight = valid[0:1] / count_row
    centered = adv[0:1] - mean_row
    grad_value_row = -value_weight * weight * adv[0:1]
    grad_out = jnp.where(
        act_rows,
        (weight * centered) * score,
        jnp.where(raw_rows == A, jnp.broadcast_to(grad_value_row, (RAW, ROWS)), 0.0),
    )
    inner = jnp.sum(grad_out * raw, axis=0, keepdims=True)
    inv = inverse[0:1]
    coef = inv * inv * inv * inner / D
    scaled_out = grad_out * inv
    tall = jnp.concatenate([scaled_out, jnp.broadcast_to(coef, (HP - RAW, ROWS))], axis=0)
    tall_rows = lax.broadcasted_iota(i32, (HP, ROWS), 0)
    tall = jnp.where(tall_rows <= RAW, tall, 0.0)
    tall_parts = parts_of(tall, 2)

    one_row = (lax.broadcasted_iota(i32, (HP, 128), 0) == RAW).astype(f32).astype(bf16)
    grad_normed = mul(tall_parts[0], heads_t[...], TN) + mul(tall_parts[1], heads_t[...], TN)
    coef_col = mul(tall_parts[0], one_row, TN) + mul(tall_parts[1], one_row, TN)
    stream = stream_s[...]
    coef_wide = jnp.concatenate([coef_col] * 4, axis=1)
    gstream[c] = (gains * grad_normed - stream * coef_wide).astype(bf16)
    send(gstream.at[c], gstream.at[c], r_g.at[0], mate)

    high, low = parts_of(stream, 2)
    q = mul(tall_parts[0], high, NN) + mul(tall_parts[0], low, NN) + mul(tall_parts[1], high, NN)
    for p in range(16):
        qsrc[p % 2, p // 2] = q[
            (p % 4) * 16 : (p % 4) * 16 + 16, (p // 4) * 128 : (p // 4) * 128 + 128
        ]
    send(qsrc.at[o], qmate, r_q0.at[0], mate)

    arrived(gstream.at[o], r_g.at[0])
    first_cols, last_cols = pl.ds(0, HALF), pl.ds(HALF, HALF)
    grads = gstream[...].reshape(2 * ROWS, COLS)
    for d in FAR_FIRST + (0,):
        zz = (z + d) % 8
        block = mul(ctx_t[zz], grads, NN).astype(bf16).reshape(2, 4, 16, COLS)
        pb[zz] = block
        if d:
            send(pb.at[zz, :, :, :, first_cols], ra.at[z], r_ra.at[z], dev(0, 0, d, c))
        else:
            ra[z] = block[:, :, :, 0:HALF]

    def to_half(rr, core):
        here = jnp.logical_and(jnp.logical_and(h == c, r == rr), c == core)
        return here, {"role": rr, "dp": z * 4 + c * 2 + core, "mp": x}

    for core in range(2):
        for rr in range(4):
            here, device = to_half(rr, core)
            send_or_keep(here, pb.at[:, core, rr, :, last_cols], rb.at[y], r_rb.at[y], device)

    arrived(qmate, r_q0.at[0])
    qsum[...] = qsrc[c] + qmate[...]
    q1[z] = qsum[z]
    for d in FAR_FIRST:
        zz = (z + d) % 8
        send(qsum.at[zz], q1.at[z], r_q1.at[z], dev(0, 0, d, c))
    for d in range(1, 8):
        zz = (z + d) % 8
        arrived(q1.at[zz], r_q1.at[zz])
    total = q1[0]
    for s in range(1, 8):
        total = total + q1[s]
    q2[y] = total
    for d in FAR_FIRST:
        send(q2.at[y], q2.at[y], r_q2.at[y], dev(0, d, 0, c))

    for d in range(1, 8):
        zz = (z + d) % 8
        arrived(ra.at[zz], r_ra.at[zz])
    total = ra[0].astype(f32)
    for s in range(1, 8):
        total = total + ra[s].astype(f32)
    sa2[...] = total
    for core in range(2):
        for rr in range(4):
            here, device = to_half(rr, core)
            send_or_keep(here, sa2.at[core, rr], ra2.at[y], r_ra2.at[y], device)
    for s in range(8):
        arrived(rb.at[s], r_rb.at[s])
    total = rb[0].astype(f32)
    for s in range(1, 8):
        total = total + rb[s].astype(f32)
    sb2[...] = total
    rb2[z] = sb2[z]
    for d in FAR_FIRST:
        send(sb2.at[(z + d) % 8], rb2.at[z], r_rb2.at[z], dev(0, 0, d, c))

    for d in range(1, 8):
        yy = (y + d) % 8
        arrived(q2.at[yy], r_q2.at[yy])
    total = q2[0]
    for s in range(1, 8):
        total = total + q2[s]
    qf[c, z] = total
    for d in FAR_FIRST:
        send(qf.at[c, z], qf.at[c, z], r_q3.at[z], dev(0, 0, d, c))

    for s in range(8):
        arrived(ra2.at[s], r_ra2.at[s])
    total = ra2[0]
    for s in range(1, 8):
        total = total + ra2[s]
    gw_out[r, :, 0:HALF] = total
    for d in range(1, 8):
        zz = (z + d) % 8
        arrived(rb2.at[zz], r_rb2.at[zz])
    total = rb2[0]
    for s in range(1, 8):
        total = total + rb2[s]
    gw_out[r, :, HALF:] = total
    for d in (2, 1, 3):
        device = {"role": (r + d) % 4, "dp": dp, "mp": x}
        send(gw_out.at[r], gw_out.at[r], r_f.at[r], device)

    for d in range(1, 8):
        zz = (z + d) % 8
        arrived(qf.at[c, zz], r_q3.at[zz])
    send(qf.at[c], qf.at[c], r_q4.at[0], mate)
    arrived(qf.at[o], r_q4.at[0])
    rows = lax.broadcasted_iota(i32, (RAW, 128), 0)
    for lane in range(4):
        cols = slice(lane * 128, lane * 128 + 128)
        block = jnp.concatenate([qf[s % 2, lane * 2 + s // 2] for s in range(3)], axis=0)
        gain_row = jnp.sum(block * heads_t[0:RAW, cols].astype(f32), axis=0, keepdims=True)
        heads_out[:, cols] = jnp.where(
            rows == A + 1, jnp.broadcast_to(gain_row, (RAW, 128)), block * gains[:, cols]
        )

    for d in range(1, 4):
        rr = (r + d) % 4
        arrived(gw_out.at[rr], r_f.at[rr])

    for condition, copy in pending:
        if condition is None:
            copy.wait_send()
        else:
            pl.when(condition)(copy.wait_send)


def finish(adv, misc, gw, heads, adv_o, mean_o, gw_o, gain_o, policy_o, value_o):
    adv_o[...] = adv[...]
    mean_o[...] = misc[0:1, 0:1]
    gw_o[...] = gw[...].reshape(64, COLS)
    gain_o[...] = heads[A + 1 : A + 2]
    policy_o[...] = heads[0:A]
    value_o[...] = heads[A : A + 1]


def per_device(
    residual_in,
    context,
    w_out,
    norm_gain,
    policy_head,
    value_head,
    rewards,
    resets,
    actions,
    lengths,
    assignment,
):
    vmem = pl.BlockSpec(memory_space=pltpu.VMEM)
    hbm = pl.BlockSpec(memory_space=pltpu.HBM)
    dma = pltpu.SemaphoreType.DMA
    buffers = [
        pltpu.VMEM((ROWS, COLS), bf16),
        pltpu.VMEM((1, COLS), f32),
        pltpu.VMEM((A, COLS), bf16),
        pltpu.VMEM((COLS,), bf16),
        pltpu.VMEM((STEPS, 32), bf16),
        pltpu.VMEM((STEPS, 32), i32),
        pltpu.VMEM((STEPS, 32), i32),
        pltpu.VMEM((1, 32), i32),
        pltpu.VMEM((1, 32), i32),
        pltpu.VMEM((4, 2, 2, ROWS, 128), bf16),
        pltpu.VMEM((8, 128, 2 * ROWS), bf16),
        pltpu.VMEM((8, 2, 64, COLS), bf16),
        pltpu.VMEM((ROWS, COLS), f32),
        pltpu.VMEM((ROWS, COLS), f32),
        pltpu.VMEM((ROWS, COLS), f32),
        pltpu.VMEM((2, ROWS, COLS), bf16),
        pltpu.VMEM((4, RAW, ROWS), f32),
        pltpu.VMEM((16, 1, 128), f32),
        pltpu.VMEM((8, 1, 128), f32),
        pltpu.VMEM((1, 128), f32),
        pltpu.VMEM((HP, COLS), bf16),
        pltpu.VMEM((2, 8, 16, 128), f32),
        pltpu.VMEM((8, 16, 128), f32),
        pltpu.VMEM((8, 16, 128), f32),
        pltpu.VMEM((8, 16, 128), f32),
        pltpu.VMEM((8, 16, 128), f32),
        pltpu.VMEM((2, 8, 16, 128), f32),
        pltpu.VMEM((8, 2, 4, 16, COLS), bf16),
        pltpu.VMEM((8, 2, 4, 16, HALF), bf16),
        pltpu.VMEM((8, 8, 16, HALF), bf16),
        pltpu.VMEM((2, 4, 16, HALF), f32),
        pltpu.VMEM((8, 16, HALF), f32),
        pltpu.VMEM((8, 16, HALF), f32),
        pltpu.VMEM((8, 16, HALF), f32),
    ]
    counts = [160, 9, 16, 16, 1, 4, 16, 8, 1, 1, 8, 8, 8, 1, 8, 8, 8, 8, 4]
    step_out = pl.pallas_call(
        kernel,
        out_shape=(
            jax.ShapeDtypeStruct((STEPS, 32), f32),
            jax.ShapeDtypeStruct((8, 128), f32),
            jax.ShapeDtypeStruct((4, 16, COLS), f32),
            jax.ShapeDtypeStruct((RAW, COLS), f32),
        ),
        in_specs=[hbm] * 11,
        out_specs=(vmem,) * 4,
        scratch_shapes=buffers + [dma((n,)) for n in counts],
        compiler_params=pltpu.CompilerParams(
            collective_id=0, has_side_effects=True, vmem_limit_bytes=62 * 1024 * 1024
        ),
        name="policy_step",
    )(
        residual_in.reshape(ROWS, COLS),
        context.reshape(ROWS, COLS),
        w_out,
        norm_gain.reshape(1, COLS),
        policy_head.T,
        value_head,
        rewards.T,
        resets.T,
        actions.T,
        lengths.reshape(1, 32),
        assignment.reshape(1, 32),
    )
    adv, mean, grad_w, grad_gain, grad_policy, grad_value = pl.pallas_call(
        finish,
        out_shape=(
            jax.ShapeDtypeStruct((STEPS, 32), f32),
            jax.ShapeDtypeStruct((1, 1), f32),
            jax.ShapeDtypeStruct((64, COLS), f32),
            jax.ShapeDtypeStruct((1, COLS), f32),
            jax.ShapeDtypeStruct((A, COLS), f32),
            jax.ShapeDtypeStruct((1, COLS), f32),
        ),
        in_specs=[vmem] * 4,
        out_specs=(vmem,) * 6,
        name="write_outputs",
    )(*step_out)
    return (
        adv.T,
        mean.reshape(1),
        grad_w,
        grad_gain.reshape(COLS),
        grad_policy.T,
        grad_value.reshape(COLS),
    )


def solution(mesh):
    placed = (
        P(("role", "dp"), None, "mp"),
        P(("role", "dp"), None, "mp"),
        P("dp", "mp"),
        P("mp"),
        P("mp", None),
        P("mp"),
        P(("role", "dp"), None),
        P(("role", "dp"), None),
        P(("role", "dp"), None),
        P(("role", "dp")),
        P(("role", "dp")),
    )
    return jax.shard_map(
        per_device,
        mesh=mesh,
        in_specs=placed,
        out_specs=(
            P(("role", "dp"), None),
            P("dp"),
            P("dp", "mp"),
            P("mp"),
            P("mp", None),
            P("mp"),
        ),
        check_vma=False,
    )
```

time: 93.8 us -> 86.5 us (0.922)
  local copies, waits for them, and re-layouts: 8.77 us -> 0 us
  Pallas kernels: 83.9 us -> 85.6 us
    unnamed x20 -> x0, local copies, waits for them, and re-layouts: 6.33 us -> none
    pallas_call x1 -> x2, Pallas kernels: 83.9 us -> 85.6 us  [the longest x1 84 us: per_device(): pl.pallas_call(kernel, out_shape=(jax.ShapeDtypeStruct((STEPS, 32), f32),...]
    slice x2 -> x0, local copies, waits for them, and re-layouts: 1.1 us -> none  [per_device(): return (adv, misc[0, 0:1], grad_w, heads[A + 1], heads[0:A].T, heads[A])]
where the time goes in v3:
time: 86.5 us; the launch traced here: 86.3 us
  Pallas kernels  85.6 us (99%)
    pallas_call x1, Pallas kernels, per_device(): pl.pallas_call(kernel, out_shape=(jax.ShapeDtypeStruct((STEPS, 32), f32),...  84 us

profile of v3, /device:TPU:1, one launch (start us, length us, event | category | flops | bytes accessed | tf_op | source)
XLA Modules:
  0.0 86.3 jit_solution(5363259441403253041)
XLA Ops:
  0.6 84.0 %policy_step.1 = (f32[8,32]{1,0:T(8,128)}, f32[8,128]{1,0:T(8,128)}, f32[4,16,512]{2,1,0:T(8,128)}, f32[48,512]{1,0:T(8,128)}) custom-call(bf16[256,512]{1,0:T(8,128)(2,1)} %bitcast.14, bf16[256,512]{1,0:T(8,128)(2,1)} %bitcast.15, bf16[64,512]{1,0:T(8,128)(2,1)} %w_h.1, f32[1,512]{1,0:T(1,128)} %bitcast.19, bf16[43,512]{1,0:T(8,128)(2,1)} %bitcast.16, ...), custom_call_target="tpu_custom_call" | custom-call | tf_op jit(solution)/shard_map/policy_step/pallas_call | solution.py:533
  84.6 1.7 %write_outputs.1 = (f32[8,32]{1,0:T(8,128)}, f32[1,1]{1,0:T(1,128)}, f32[64,512]{1,0:T(8,128)}, f32[1,512]{1,0:T(1,128)}, f32[43,512]{1,0:T(8,128)}, /*index=5*/f32[1,512]{1,0:T(1,128)}) custom-call(f32[8,32]{1,0:T(8,128)} %get-tuple-element.16.adv, f32[8,128]{1,0:T(8,128)} %get-tuple-element.17.misc, f32[4,16,512]{2,1,0:T(8,128)} %get-tuple-element.18.gw, ...), custom_call_target="tpu_custom_call" | custom-call | tf_op jit(solution)/shard_map/write_outputs/pallas_call | solution.py:561

commit v4 on v3

--- a/solution.py
+++ b/solution.py
@@ -53,7 +53,7 @@
     ctxbuf, ctx_t, wbuf, psend, precv, stream_s, gstream,
     rawbuf, l1, l2, lsrc, heads_t, qsrc, qmate, qsum, q1, q2, qf,
     pb, ra, rb, sa2, sb2, ra2, rb2,
-    s_all, r_in, r_ctx, r_w, r_p, r_raw, r_l1, r_l2, r_g,
+    s_all, r_in, r_ctx, r_w, r_wy, r_p, r_raw, r_l1, r_l2, r_g,
     r_q0, r_q1, r_q2, r_q3, r_q4, r_ra, r_rb, r_ra2, r_rb2, r_f,
 ):
     role = lax.axis_index("role")
@@ -121,16 +121,20 @@
 
     barrier = pltpu.get_barrier_semaphore()
     peers = [mate, dev(1, 0, 0, 0), dev(1, 0, 0, 1), dev(3, 0, 0, 0), dev(3, 0, 0, 1)]
-    peers += [dev(0, 0, 1, c), dev(0, 0, 7, c)]
+    peers += [dev(0, 0, d, c) for d in (1, 2, 6, 7)]
     peers += [dev(0, d, 0, c) for d in range(1, 8)]
     peers += [{"role": 3 - r, "dp": z * 4 + (1 - h) * 2 + o, "mp": x}]
     for peer in peers:
         pl.semaphore_signal(barrier, inc=1, device_id=peer, device_id_type=MESH)
     pl.semaphore_wait(barrier, len(peers))
 
-    send_or_keep(c == h, w_h, wbuf.at[z, c], r_w.at[z * 2 + c], mate)
+    mine = pl.ds(pl.multiple_of((y % 2) * HALF, HALF), HALF)
+    theirs = pl.ds(pl.multiple_of((1 - y % 2) * HALF, HALF), HALF)
     mirror = {"role": 3 - r, "dp": z * 4 + (1 - h) * 2 + h, "mp": x}
-    send(w_h, wbuf.at[z, c], r_w.at[z * 2 + c], mirror)
+    send(w_h.at[:, :, theirs], wbuf.at[z, c, :, :, theirs], r_w.at[z * 2 + c], mirror)
+    send_or_keep(
+        c == h, w_h.at[:, :, mine], wbuf.at[z, c, :, :, mine], r_w.at[z * 2 + c], mate
+    )
 
     def piece(zz, core):
         return ctx_h.at[:, pl.ds(pl.multiple_of(zz * 256 + core * 128, 128), 128)]
@@ -146,16 +150,19 @@
         pltpu.make_async_copy(piece(zz, c), ctxbuf.at[x, c, zz], ctx_sem(x, c, zz)).start()
         send(piece(zz, o), ctxbuf.at[x, c, zz], ctx_sem(x, c, zz), mate)
 
-    up, down = dev(0, 0, 1, c), dev(0, 0, 7, c)
-
     def w_block(zz, cc):
-        return wbuf.at[zz, cc], r_w.at[zz * 2 + cc]
+        return wbuf.at[zz, cc, :, :, mine], r_w.at[zz * 2 + cc]
+
+    def to_y(zz, cc):
+        block = wbuf.at[zz, cc, :, :, mine]
+        send(block, block, r_wy.at[zz * 2 + cc], dev(0, 1 if cc == 0 else 7, 0, c))
 
     for cc in range(2):
         block, sem = w_block(z, cc)
         arrived(block, sem)
-        send(block, block, sem, up)
-        send(block, block, sem, down)
+        for d in (2, 6, 1, 7):
+            send(block, block, sem, dev(0, 0, d, c))
+        to_y(z, cc)
 
     for n in range(9):
         pltpu.make_async_copy(small[n][0], small[n][1], r_in.at[n]).wait()
@@ -194,14 +201,23 @@
             arrived(block, ctx_sem(m, cc, zz))
             send(block, block, ctx_sem(m, cc, zz), dev(dx, 0, 0, c))
 
-    for s in range(1, 5):
+    for cc in range(2):
+        for d in (6, 2):
+            block, sem = w_block((z + d) % 8, cc)
+            arrived(block, sem)
+            if d == 6:
+                if cc == 0:
+                    send(block, block, sem, dev(0, 0, 2, c))
+                send(block, block, sem, dev(0, 0, 1, c))
+            else:
+                if cc == 1:
+                    send(block, block, sem, dev(0, 0, 6, c))
+                send(block, block, sem, dev(0, 0, 7, c))
+            to_y((z + d) % 8, cc)
+    for d in (1, 7, 3, 5, 4):
         for cc in range(2):
-            for sign, target, most in ((-1, up, 4 - cc), (1, down, 3 + cc)):
-                if s <= most:
-                    block, sem = w_block((z + sign * s + 8) % 8, cc)
-                    arrived(block, sem)
-                    if s < most:
-                        send(block, block, sem, target)
+            arrived(*w_block((z + d) % 8, cc))
+            to_y((z + d) % 8, cc)
 
     for cc in range(2):
         for zz in range(2):
@@ -212,6 +228,9 @@
         arrived(ctxbuf.at[m, cc, 1], ctx_sem(m, cc, 1))
         m = (x + 1) % 4
         arrived(ctxbuf.at[m, cc, 0], ctx_sem(m, cc, 0))
+    for s in range(8):
+        for cc in range(2):
+            arrived(wbuf.at[s, cc, :, :, theirs], r_wy.at[s * 2 + cc])
 
     def project(core):
         total = None
@@ -358,6 +377,13 @@
         ]
     send(qsrc.at[o], qmate, r_q0.at[0], mate)
 
+    arrived(qmate, r_q0.at[0])
+    qsum[...] = qsrc[c] + qmate[...]
+    q1[z] = qsum[z]
+    for d in FAR_FIRST:
+        zz = (z + d) % 8
+        send(qsum.at[zz], q1.at[z], r_q1.at[z], dev(0, 0, d, c))
+
     arrived(gstream.at[o], r_g.at[0])
     first_cols, last_cols = pl.ds(0, HALF), pl.ds(HALF, HALF)
     grads = gstream[...].reshape(2 * ROWS, COLS)
@@ -379,12 +405,6 @@
             here, device = to_half(rr, core)
             send_or_keep(here, pb.at[:, core, rr, :, last_cols], rb.at[y], r_rb.at[y], device)
 
-    arrived(qmate, r_q0.at[0])
-    qsum[...] = qsrc[c] + qmate[...]
-    q1[z] = qsum[z]
-    for d in FAR_FIRST:
-        zz = (z + d) % 8
-        send(qsum.at[zz], q1.at[z], r_q1.at[z], dev(0, 0, d, c))
     for d in range(1, 8):
         zz = (z + d) % 8
         arrived(q1.at[zz], r_q1.at[zz])
@@ -505,7 +525,7 @@
         pltpu.VMEM((1, 32), i32),
         pltpu.VMEM((4, 2, 2, ROWS, 128), bf16),
         pltpu.VMEM((8, 128, 2 * ROWS), bf16),
-        pltpu.VMEM((8, 2, 64, COLS), bf16),
+        pltpu.VMEM((8, 2, 4, 16, COLS), bf16),
         pltpu.VMEM((ROWS, COLS), f32),
         pltpu.VMEM((ROWS, COLS), f32),
         pltpu.VMEM((ROWS, COLS), f32),
@@ -529,7 +549,7 @@
         pltpu.VMEM((8, 16, HALF), f32),
         pltpu.VMEM((8, 16, HALF), f32),
     ]
-    counts = [160, 9, 16, 16, 1, 4, 16, 8, 1, 1, 8, 8, 8, 1, 8, 8, 8, 8, 4]
+    counts = [160, 9, 16, 16, 16, 1, 4, 16, 8, 1, 1, 8, 8, 8, 1, 8, 8, 8, 8, 4]
     step_out = pl.pallas_call(
         kernel,
         out_shape=(
@@ -548,7 +568,7 @@
     )(
         residual_in.reshape(ROWS, COLS),
         context.reshape(ROWS, COLS),
-        w_out,
+        w_out.reshape(4, 16, COLS),
         norm_gain.reshape(1, COLS),
         policy_head.T,
         value_head,

time: 86.5 us -> 82 us (0.948)
  Pallas kernels: 85.6 us -> 81.2 us
    pallas_call x1, Pallas kernels: 84 us -> 79.5 us  [per_device(): pl.pallas_call(kernel, out_shape=(jax.ShapeDtypeStruct((STEPS, 32), f32),...]
where the time goes in v4:
time: 82 us; the launch traced here: 81.8 us
  Pallas kernels  81.2 us (99%)
    pallas_call x1, Pallas kernels, per_device(): pl.pallas_call(kernel, out_shape=(jax.ShapeDtypeStruct((STEPS, 32), f32),...  79.5 us
    pallas_call x1, Pallas kernels, per_device(): pl.pallas_call(finish, out_shape=(jax.ShapeDtypeStruct((STEPS, 32), f32),...  1.67 us

profile of v4, /device:TPU:1, one launch (start us, length us, event | category | flops | bytes accessed | tf_op | source)
XLA Modules:
  0.0 81.8 jit_solution(5166268564894444338)
XLA Ops:
  0.6 79.5 %policy_step.1 = (f32[8,32]{1,0:T(8,128)}, f32[8,128]{1,0:T(8,128)}, f32[4,16,512]{2,1,0:T(8,128)}, f32[48,512]{1,0:T(8,128)}) custom-call(bf16[256,512]{1,0:T(8,128)(2,1)} %bitcast.15, bf16[256,512]{1,0:T(8,128)(2,1)} %bitcast.16, bf16[4,16,512]{2,1,0:T(8,128)(2,1)} %bitcast.17, f32[1,512]{1,0:T(1,128)} %bitcast.21, bf16[43,512]{1,0:T(8,128)(2,1)} %bitcast.18, ...), custom_call_target="tpu_custom_call" | custom-call | tf_op jit(solution)/shard_map/policy_step/pallas_call | solution.py:553
  80.2 1.7 %write_outputs.1 = (f32[8,32]{1,0:T(8,128)}, f32[1,1]{1,0:T(1,128)}, f32[64,512]{1,0:T(8,128)}, f32[1,512]{1,0:T(1,128)}, f32[43,512]{1,0:T(8,128)}, /*index=5*/f32[1,512]{1,0:T(1,128)}) custom-call(f32[8,32]{1,0:T(8,128)} %get-tuple-element.16.adv, f32[8,128]{1,0:T(8,128)} %get-tuple-element.17.misc, f32[4,16,512]{2,1,0:T(8,128)} %get-tuple-element.18.gw, ...), custom_call_target="tpu_custom_call" | custom-call | tf_op jit(solution)/shard_map/write_outputs/pallas_call | solution.py:581

commit v5 on v4

--- a/solution.py
+++ b/solution.py
@@ -54,7 +54,7 @@
     rawbuf, l1, l2, lsrc, heads_t, qsrc, qmate, qsum, q1, q2, qf,
     pb, ra, rb, sa2, sb2, ra2, rb2,
     s_all, r_in, r_ctx, r_w, r_wy, r_p, r_raw, r_l1, r_l2, r_g,
-    r_q0, r_q1, r_q2, r_q3, r_q4, r_ra, r_rb, r_ra2, r_rb2, r_f,
+    r_q0, r_q1, r_q2, r_q3, r_q4, r_ra, r_rb, r_ra2, r_rb2, r_f, tokens,
 ):
     role = lax.axis_index("role")
     dp = lax.axis_index("dp")
@@ -122,11 +122,23 @@
     barrier = pltpu.get_barrier_semaphore()
     peers = [mate, dev(1, 0, 0, 0), dev(1, 0, 0, 1), dev(3, 0, 0, 0), dev(3, 0, 0, 1)]
     peers += [dev(0, 0, d, c) for d in (1, 2, 6, 7)]
-    peers += [dev(0, d, 0, c) for d in range(1, 8)]
-    peers += [{"role": 3 - r, "dp": z * 4 + (1 - h) * 2 + o, "mp": x}]
+    peers += [dev(0, 1, 0, c), dev(0, 7, 0, c)]
+    peers += [{"role": 3 - r, "dp": z * 4 + (1 - h) * 2 + core, "mp": x} for core in range(2)]
     for peer in peers:
         pl.semaphore_signal(barrier, inc=1, device_id=peer, device_id_type=MESH)
     pl.semaphore_wait(barrier, len(peers))
+
+    def tell(n):
+        pl.semaphore_signal(tokens.at[2 * n], inc=1, device_id=dev(0, 1, 0, c), device_id_type=MESH)
+        pl.semaphore_signal(
+            tokens.at[2 * n + 1], inc=1, device_id=dev(0, 7, 0, c), device_id_type=MESH
+        )
+
+    def hear(n):
+        pl.semaphore_wait(tokens.at[2 * n], 1)
+        pl.semaphore_wait(tokens.at[2 * n + 1], 1)
+
+    tell(0)
 
     mine = pl.ds(pl.multiple_of((y % 2) * HALF, HALF), HALF)
     theirs = pl.ds(pl.multiple_of((1 - y % 2) * HALF, HALF), HALF)
@@ -201,6 +213,8 @@
             arrived(block, ctx_sem(m, cc, zz))
             send(block, block, ctx_sem(m, cc, zz), dev(dx, 0, 0, c))
 
+    hear(0)
+    tell(1)
     for cc in range(2):
         for d in (6, 2):
             block, sem = w_block((z + d) % 8, cc)
@@ -214,6 +228,8 @@
                     send(block, block, sem, dev(0, 0, 6, c))
                 send(block, block, sem, dev(0, 0, 7, c))
             to_y((z + d) % 8, cc)
+    hear(1)
+    tell(2)
     for d in (1, 7, 3, 5, 4):
         for cc in range(2):
             arrived(*w_block((z + d) % 8, cc))
@@ -228,6 +244,7 @@
         arrived(ctxbuf.at[m, cc, 1], ctx_sem(m, cc, 1))
         m = (x + 1) % 4
         arrived(ctxbuf.at[m, cc, 0], ctx_sem(m, cc, 0))
+    hear(2)
     for s in range(8):
         for cc in range(2):
             arrived(wbuf.at[s, cc, :, :, theirs], r_wy.at[s * 2 + cc])
@@ -396,6 +413,16 @@
         else:
             ra[z] = block[:, :, :, 0:HALF]
 
+    def gather_sum(buf, sems, own, wait_own):
+        if wait_own:
+            arrived(buf.at[own], sems.at[own])
+        total = buf[own].astype(f32)
+        for d in (1, 7, 2, 6, 3, 5, 4):
+            n = (own + d) % 8
+            arrived(buf.at[n], sems.at[n])
+            total = total + buf[n].astype(f32)
+        return total
+
     def to_half(rr, core):
         here = jnp.logical_and(jnp.logical_and(h == c, r == rr), c == core)
         return here, {"role": rr, "dp": z * 4 + c * 2 + core, "mp": x}
@@ -415,23 +442,12 @@
     for d in FAR_FIRST:
         send(q2.at[y], q2.at[y], r_q2.at[y], dev(0, d, 0, c))
 
-    for d in range(1, 8):
-        zz = (z + d) % 8
-        arrived(ra.at[zz], r_ra.at[zz])
-    total = ra[0].astype(f32)
-    for s in range(1, 8):
-        total = total + ra[s].astype(f32)
-    sa2[...] = total
+    sa2[...] = gather_sum(ra, r_ra, z, False)
     for core in range(2):
         for rr in range(4):
             here, device = to_half(rr, core)
             send_or_keep(here, sa2.at[core, rr], ra2.at[y], r_ra2.at[y], device)
-    for s in range(8):
-        arrived(rb.at[s], r_rb.at[s])
-    total = rb[0].astype(f32)
-    for s in range(1, 8):
-        total = total + rb[s].astype(f32)
-    sb2[...] = total
+    sb2[...] = gather_sum(rb, r_rb, y, True)
     rb2[z] = sb2[z]
     for d in FAR_FIRST:
         send(sb2.at[(z + d) % 8], rb2.at[z], r_rb2.at[z], dev(0, 0, d, c))
@@ -446,22 +462,16 @@
     for d in FAR_FIRST:
         send(qf.at[c, z], qf.at[c, z], r_q3.at[z], dev(0, 0, d, c))
 
-    for s in range(8):
-        arrived(ra2.at[s], r_ra2.at[s])
-    total = ra2[0]
-    for s in range(1, 8):
-        total = total + ra2[s]
-    gw_out[r, :, 0:HALF] = total
-    for d in range(1, 8):
-        zz = (z + d) % 8
-        arrived(rb2.at[zz], r_rb2.at[zz])
-    total = rb2[0]
-    for s in range(1, 8):
-        total = total + rb2[s]
-    gw_out[r, :, HALF:] = total
-    for d in (2, 1, 3):
-        device = {"role": (r + d) % 4, "dp": dp, "mp": x}
-        send(gw_out.at[r], gw_out.at[r], r_f.at[r], device)
+    def to_roles(part, cols):
+        for d in (2, 1, 3):
+            device = {"role": (r + d) % 4, "dp": dp, "mp": x}
+            block = gw_out.at[r, :, cols]
+            send(block, block, r_f.at[part * 4 + r], device)
+
+    gw_out[r, :, 0:HALF] = gather_sum(ra2, r_ra2, y, True)
+    to_roles(0, first_cols)
+    gw_out[r, :, HALF:] = gather_sum(rb2, r_rb2, z, False)
+    to_roles(1, last_cols)
 
     for d in range(1, 8):
         zz = (z + d) % 8
@@ -479,7 +489,8 @@
 
     for d in range(1, 4):
         rr = (r + d) % 4
-        arrived(gw_out.at[rr], r_f.at[rr])
+        arrived(gw_out.at[rr, :, first_cols], r_f.at[rr])
+        arrived(gw_out.at[rr, :, last_cols], r_f.at[4 + rr])
 
     for condition, copy in pending:
         if condition is None:
@@ -549,7 +560,7 @@
         pltpu.VMEM((8, 16, HALF), f32),
         pltpu.VMEM((8, 16, HALF), f32),
     ]
-    counts = [160, 9, 16, 16, 16, 1, 4, 16, 8, 1, 1, 8, 8, 8, 1, 8, 8, 8, 8, 4]
+    counts = [160, 9, 16, 16, 16, 1, 4, 16, 8, 1, 1, 8, 8, 8, 1, 8, 8, 8, 8, 8]
     step_out = pl.pallas_call(
         kernel,
         out_shape=(
@@ -560,7 +571,9 @@
         ),
         in_specs=[hbm] * 11,
         out_specs=(vmem,) * 4,
-        scratch_shapes=buffers + [dma((n,)) for n in counts],
+        scratch_shapes=buffers
+        + [dma((n,)) for n in counts]
+        + [pltpu.SemaphoreType.REGULAR((6,))],
         compiler_params=pltpu.CompilerParams(
             collective_id=0, has_side_effects=True, vmem_limit_bytes=62 * 1024 * 1024
         ),

time: 82 us -> 81.5 us (level)
  no operation moved by 1% of the time
where the time goes in v5:
time: 81.5 us; the launch traced here: 81.3 us
  Pallas kernels  80.7 us (99%)
    pallas_call x1, Pallas kernels, per_device(): pl.pallas_call(kernel, out_shape=(jax.ShapeDtypeStruct((STEPS, 32), f32),...  79 us
    pallas_call x1, Pallas kernels, per_device(): pl.pallas_call(finish, out_shape=(jax.ShapeDtypeStruct((STEPS, 32), f32),...  1.67 us

profile of v5, /device:TPU:1, one launch (start us, length us, event | category | flops | bytes accessed | tf_op | source)
XLA Modules:
  0.0 81.3 jit_solution(12187449341393789843)
XLA Ops:
  0.6 79.0 %policy_step.1 = (f32[8,32]{1,0:T(8,128)}, f32[8,128]{1,0:T(8,128)}, f32[4,16,512]{2,1,0:T(8,128)}, f32[48,512]{1,0:T(8,128)}) custom-call(bf16[256,512]{1,0:T(8,128)(2,1)} %bitcast.15, bf16[256,512]{1,0:T(8,128)(2,1)} %bitcast.16, bf16[4,16,512]{2,1,0:T(8,128)(2,1)} %bitcast.17, f32[1,512]{1,0:T(1,128)} %bitcast.21, bf16[43,512]{1,0:T(8,128)(2,1)} %bitcast.18, ...), custom_call_target="tpu_custom_call" | custom-call | tf_op jit(solution)/shard_map/policy_step/pallas_call | solution.py:564
  79.7 1.7 %write_outputs.1 = (f32[8,32]{1,0:T(8,128)}, f32[1,1]{1,0:T(1,128)}, f32[64,512]{1,0:T(8,128)}, f32[1,512]{1,0:T(1,128)}, f32[43,512]{1,0:T(8,128)}, /*index=5*/f32[1,512]{1,0:T(1,128)}) custom-call(f32[8,32]{1,0:T(8,128)} %get-tuple-element.16.adv, f32[8,128]{1,0:T(8,128)} %get-tuple-element.17.misc, f32[4,16,512]{2,1,0:T(8,128)} %get-tuple-element.18.gw, ...), custom_call_target="tpu_custom_call" | custom-call | tf_op jit(solution)/shard_map/write_outputs/pallas_call | solution.py:594

commit v6 on v5

--- a/solution.py
+++ b/solution.py
@@ -94,6 +94,11 @@
         copy.start()
         pending.append((None, copy))
 
+    def send_when(condition, src, dst, rsem, device):
+        copy = remote(src, dst, rsem, device)
+        pl.when(condition)(copy.start)
+        pending.append((condition, copy))
+
     def send_or_keep(here, src, dst, rsem, device):
         copy = remote(src, dst, rsem, device)
         away = jnp.logical_not(here)
@@ -123,10 +128,12 @@
     peers = [mate, dev(1, 0, 0, 0), dev(1, 0, 0, 1), dev(3, 0, 0, 0), dev(3, 0, 0, 1)]
     peers += [dev(0, 0, d, c) for d in (1, 2, 6, 7)]
     peers += [dev(0, 1, 0, c), dev(0, 7, 0, c)]
-    peers += [{"role": 3 - r, "dp": z * 4 + (1 - h) * 2 + core, "mp": x} for core in range(2)]
+    source = 3 * (1 - r // 2)
+    peers += [{"role": source, "dp": z * 4 + (1 - h) * 2 + core, "mp": x} for core in range(2)]
+    border = r % 3 == 0
     for peer in peers:
         pl.semaphore_signal(barrier, inc=1, device_id=peer, device_id_type=MESH)
-    pl.semaphore_wait(barrier, len(peers))
+    pl.semaphore_wait(barrier, len(peers) - 2 + jnp.where(border, 4, 0))
 
     def tell(n):
         pl.semaphore_signal(tokens.at[2 * n], inc=1, device_id=dev(0, 1, 0, c), device_id_type=MESH)
@@ -142,8 +149,13 @@
 
     mine = pl.ds(pl.multiple_of((y % 2) * HALF, HALF), HALF)
     theirs = pl.ds(pl.multiple_of((1 - y % 2) * HALF, HALF), HALF)
-    mirror = {"role": 3 - r, "dp": z * 4 + (1 - h) * 2 + h, "mp": x}
-    send(w_h.at[:, :, theirs], wbuf.at[z, c, :, :, theirs], r_w.at[z * 2 + c], mirror)
+    for n in range(2):
+        to_role = jnp.where(r == 3, n, 3 - n)
+        cols = pl.ds(pl.multiple_of((to_role % 2) * HALF, HALF), HALF)
+        across = {"role": to_role, "dp": z * 4 + (1 - h) * 2 + h, "mp": x}
+        send_when(
+            border, w_h.at[:, :, cols], wbuf.at[z, c, :, :, cols], r_w.at[z * 2 + c], across
+        )
     send_or_keep(
         c == h, w_h.at[:, :, mine], wbuf.at[z, c, :, :, mine], r_w.at[z * 2 + c], mate
     )
@@ -423,14 +435,19 @@
             total = total + buf[n].astype(f32)
         return total
 
-    def to_half(rr, core):
-        here = jnp.logical_and(jnp.logical_and(h == c, r == rr), c == core)
-        return here, {"role": rr, "dp": z * 4 + c * 2 + core, "mp": x}
-
-    for core in range(2):
-        for rr in range(4):
-            here, device = to_half(rr, core)
-            send_or_keep(here, pb.at[:, core, rr, :, last_cols], rb.at[y], r_rb.at[y], device)
+    def to_half(block_of, dst, rsem):
+        for n in (2, 1, 3, 0):
+            rr = (r + n) % 4
+            for core in range(2):
+                block = block_of(core, rr)
+                device = {"role": rr, "dp": z * 4 + c * 2 + core, "mp": x}
+                if n:
+                    send(block, dst, rsem, device)
+                else:
+                    here = jnp.logical_and(h == c, c == core)
+                    send_or_keep(here, block, dst, rsem, device)
+
+    to_half(lambda core, rr: pb.at[:, core, rr, :, last_cols], rb.at[y], r_rb.at[y])
 
     for d in range(1, 8):
         zz = (z + d) % 8
@@ -443,10 +460,7 @@
         send(q2.at[y], q2.at[y], r_q2.at[y], dev(0, d, 0, c))
 
     sa2[...] = gather_sum(ra, r_ra, z, False)
-    for core in range(2):
-        for rr in range(4):
-            here, device = to_half(rr, core)
-            send_or_keep(here, sa2.at[core, rr], ra2.at[y], r_ra2.at[y], device)
+    to_half(lambda core, rr: sa2.at[core, rr], ra2.at[y], r_ra2.at[y])
     sb2[...] = gather_sum(rb, r_rb, y, True)
     rb2[z] = sb2[z]
     for d in FAR_FIRST:

time: 81.5 us -> 80.7 us (level)
  Pallas kernels: 80.7 us -> 79.8 us
    pallas_call x1, Pallas kernels: 79 us -> 78.2 us  [per_device(): pl.pallas_call(kernel, out_shape=(jax.ShapeDtypeStruct((STEPS, 32), f32),...]
where the time goes in v6:
time: 80.7 us; the launch traced here: 80.5 us
  Pallas kernels  79.8 us (99%)
    pallas_call x1, Pallas kernels, per_device(): pl.pallas_call(kernel, out_shape=(jax.ShapeDtypeStruct((STEPS, 32), f32),...  78.2 us
    pallas_call x1, Pallas kernels, per_device(): pl.pallas_call(finish, out_shape=(jax.ShapeDtypeStruct((STEPS, 32), f32),...  1.67 us

profile of v6, /device:TPU:1, one launch (start us, length us, event | category | flops | bytes accessed | tf_op | source)
XLA Modules:
  0.0 80.5 jit_solution(10182701239752614451)
XLA Ops:
  0.6 78.2 %policy_step.1 = (f32[8,32]{1,0:T(8,128)}, f32[8,128]{1,0:T(8,128)}, f32[4,16,512]{2,1,0:T(8,128)}, f32[48,512]{1,0:T(8,128)}) custom-call(bf16[256,512]{1,0:T(8,128)(2,1)} %bitcast.15, bf16[256,512]{1,0:T(8,128)(2,1)} %bitcast.16, bf16[4,16,512]{2,1,0:T(8,128)(2,1)} %bitcast.17, f32[1,512]{1,0:T(1,128)} %bitcast.21, bf16[43,512]{1,0:T(8,128)(2,1)} %bitcast.18, ...), custom_call_target="tpu_custom_call" | custom-call | tf_op jit(solution)/shard_map/policy_step/pallas_call | solution.py:578
  78.8 1.7 %write_outputs.1 = (f32[8,32]{1,0:T(8,128)}, f32[1,1]{1,0:T(1,128)}, f32[64,512]{1,0:T(8,128)}, f32[1,512]{1,0:T(1,128)}, f32[43,512]{1,0:T(8,128)}, /*index=5*/f32[1,512]{1,0:T(1,128)}) custom-call(f32[8,32]{1,0:T(8,128)} %get-tuple-element.16.adv, f32[8,128]{1,0:T(8,128)} %get-tuple-element.17.misc, f32[4,16,512]{2,1,0:T(8,128)} %get-tuple-element.18.gw, ...), custom_call_target="tpu_custom_call" | custom-call | tf_op jit(solution)/shard_map/write_outputs/pallas_call | solution.py:608

commit v7 on v6

--- a/solution.py
+++ b/solution.py
@@ -409,9 +409,18 @@
     arrived(qmate, r_q0.at[0])
     qsum[...] = qsrc[c] + qmate[...]
     q1[z] = qsum[z]
+
+    def filled(zz):
+        return jnp.logical_or(c == 0, zz % 2 == 0)
+
+    def arrived_when(condition, dst, rsem):
+        @pl.when(condition)
+        def _():
+            arrived(dst, rsem)
+
     for d in FAR_FIRST:
         zz = (z + d) % 8
-        send(qsum.at[zz], q1.at[z], r_q1.at[z], dev(0, 0, d, c))
+        send_when(filled(zz), qsum.at[zz], q1.at[z], r_q1.at[z], dev(0, 0, d, c))
 
     arrived(gstream.at[o], r_g.at[0])
     first_cols, last_cols = pl.ds(0, HALF), pl.ds(HALF, HALF)
@@ -451,13 +460,13 @@
 
     for d in range(1, 8):
         zz = (z + d) % 8
-        arrived(q1.at[zz], r_q1.at[zz])
+        arrived_when(filled(z), q1.at[zz], r_q1.at[zz])
     total = q1[0]
     for s in range(1, 8):
         total = total + q1[s]
     q2[y] = total
     for d in FAR_FIRST:
-        send(q2.at[y], q2.at[y], r_q2.at[y], dev(0, d, 0, c))
+        send_when(filled(z), q2.at[y], q2.at[y], r_q2.at[y], dev(0, d, 0, c))
 
     sa2[...] = gather_sum(ra, r_ra, z, False)
     to_half(lambda core, rr: sa2.at[core, rr], ra2.at[y], r_ra2.at[y])
@@ -468,13 +477,13 @@
 
     for d in range(1, 8):
         yy = (y + d) % 8
-        arrived(q2.at[yy], r_q2.at[yy])
+        arrived_when(filled(z), q2.at[yy], r_q2.at[yy])
     total = q2[0]
     for s in range(1, 8):
         total = total + q2[s]
     qf[c, z] = total
     for d in FAR_FIRST:
-        send(qf.at[c, z], qf.at[c, z], r_q3.at[z], dev(0, 0, d, c))
+        send_when(filled(z), qf.at[c, z], qf.at[c, z], r_q3.at[z], dev(0, 0, d, c))
 
     def to_roles(part, cols):
         for d in (2, 1, 3):
@@ -489,7 +498,7 @@
 
     for d in range(1, 8):
         zz = (z + d) % 8
-        arrived(qf.at[c, zz], r_q3.at[zz])
+        arrived_when(filled(zz), qf.at[c, zz], r_q3.at[zz])
     send(qf.at[c], qf.at[c], r_q4.at[0], mate)
     arrived(qf.at[o], r_q4.at[0])
     rows = lax.broadcasted_iota(i32, (RAW, 128), 0)

time: 80.7 us -> 80.5 us (level)
  no operation moved by 1% of the time
where the time goes in v7:
time: 80.5 us; the launch traced here: 80.3 us
  Pallas kernels  79.6 us (99%)
    pallas_call x1, Pallas kernels, per_device(): pl.pallas_call(kernel, out_shape=(jax.ShapeDtypeStruct((STEPS, 32), f32),...  78 us
    pallas_call x1, Pallas kernels, per_device(): pl.pallas_call(finish, out_shape=(jax.ShapeDtypeStruct((STEPS, 32), f32),...  1.67 us

profile of v7, /device:TPU:1, one launch (start us, length us, event | category | flops | bytes accessed | tf_op | source)
XLA Modules:
  0.0 80.3 jit_solution(3288037782456825336)
XLA Ops:
  0.6 78.0 %policy_step.1 = (f32[8,32]{1,0:T(8,128)}, f32[8,128]{1,0:T(8,128)}, f32[4,16,512]{2,1,0:T(8,128)}, f32[48,512]{1,0:T(8,128)}) custom-call(bf16[256,512]{1,0:T(8,128)(2,1)} %bitcast.15, bf16[256,512]{1,0:T(8,128)(2,1)} %bitcast.16, bf16[4,16,512]{2,1,0:T(8,128)(2,1)} %bitcast.17, f32[1,512]{1,0:T(1,128)} %bitcast.21, bf16[43,512]{1,0:T(8,128)(2,1)} %bitcast.18, ...), custom_call_target="tpu_custom_call" | custom-call | tf_op jit(solution)/shard_map/policy_step/pallas_call | solution.py:587
  78.6 1.7 %write_outputs.1 = (f32[8,32]{1,0:T(8,128)}, f32[1,1]{1,0:T(1,128)}, f32[64,512]{1,0:T(8,128)}, f32[1,512]{1,0:T(1,128)}, f32[43,512]{1,0:T(8,128)}, /*index=5*/f32[1,512]{1,0:T(1,128)}) custom-call(f32[8,32]{1,0:T(8,128)} %get-tuple-element.16.adv, f32[8,128]{1,0:T(8,128)} %get-tuple-element.17.misc, f32[4,16,512]{2,1,0:T(8,128)} %get-tuple-element.18.gw, ...), custom_call_target="tpu_custom_call" | custom-call | tf_op jit(solution)/shard_map/write_outputs/pallas_call | solution.py:617
